TPU v7x, 32 devices: a whole 2x2x4 slice. The times are simulated.
32 devices in a mesh: win: 16 (over z, y, x), state: 2 (over core).
Axes of the slice: x: 2, y: 2, z: 4, core: 2. Of those that a mesh axis runs over, the one named last changes fastest.
Arguments:
- anomalies: float32 [16, 512, 256], P('win', 'state'), may hold values from -12 to 12
- mean_state: float32 [16, 512], P('win', 'state'), may hold values from -6 to 6
- obs_rows: int32 [16, 256], P('win', 'state'), may hold values from 0 to 255
- obs_precision: float32 [16, 256], P('win', 'state'), may hold values from 0.03125 to 0.3125
Outputs:
- updated: float32 [16, 512, 256], P('win', 'state')
Inputs may be any that keep to these rules, and one draw needn't show every extreme that they name: Observation j of window w reads state row (j // 128) * 256 + obs_rows[w, j], a row of the same block of 256 rows.
All inputs are finite; a program needn't handle non-finite values.
Results may differ from a plain program's by a relative error of at most 0.0003.
Values sent between devices are 32-bit elements; how exact they have to be, the bound alone decides.
A program may use at most 128 MiB of HBM per device.

v0:
```python
import jax
import jax.numpy as jnp
from jax import lax
from jax.sharding import PartitionSpec as P

NS_STEPS = 3


PRECISE = lax.Precision.HIGHEST


def passed_along(x, axis, by):
    count = lax.axis_size(axis)
    pairs = [(i, i + by) for i in range(count) if 0 <= i + by < count]
    return lax.ppermute(x, axis, pairs)


def high_dot(left, right):
    return jnp.dot(left, right, precision=PRECISE, preferred_element_type=jnp.float32)


def inverse_root(gram_matrix):
    members = gram_matrix.shape[0]
    unit_matrix = jnp.eye(members, dtype=jnp.float32)
    system = unit_matrix + gram_matrix
    frob_scale = jnp.sqrt(jnp.sum(system * system))
    root_iter = system / frob_scale
    factor = 1.5 * unit_matrix - 0.5 * root_iter
    inverse = factor
    root_iter = high_dot(root_iter, factor)
    for ns_index in range(1, NS_STEPS):
        factor = 1.5 * unit_matrix - 0.5 * high_dot(inverse, root_iter)
        if ns_index + 1 < NS_STEPS:
            root_iter = high_dot(root_iter, factor)
        inverse = high_dot(factor, inverse)
    return inverse * (members / jnp.trace(inverse))


def gram_terms(current, mean_state, obs_rows, obs_precision):
    row_count = current.shape[1]
    members = current.shape[2]
    positions = jnp.arange(row_count, dtype=jnp.int32)
    selector = (obs_rows[:, :, None] == positions[None, None, :]).astype(jnp.float32)
    picked = jnp.einsum("wor,wrm->wom", selector, current, precision=PRECISE)
    base_value = jnp.einsum("wor,wr->wo", selector, mean_state, precision=PRECISE)
    predicted = jnp.tanh(base_value[:, :, None] + picked)
    centred = (predicted - jnp.mean(predicted, axis=2, keepdims=True)) * jnp.sqrt(obs_precision)[
        :, :, None
    ]
    return jnp.einsum("wom,won->wmn", centred, centred, precision=PRECISE) / (members - 1)


def rows_suffix(device_total, unit_matrix):
    state_parts = lax.axis_size("state")
    block_rows = device_total.shape[0] // state_parts
    first_row = lax.axis_index("state") * block_rows
    covered = lax.dynamic_slice_in_dim(device_total, first_row, block_rows, 0)
    length = lax.axis_size("win")
    position = lax.axis_index("win")
    for level_index in range((length - 1).bit_length()):
        stride = 1 << level_index
        received = passed_along(covered, "win", -stride)
        partner = lax.all_gather(received, "state", axis=0, tiled=True)
        covered = jnp.where(position + stride < length, high_dot(covered, partner), covered)
    following = passed_along(covered, "win", -1)
    own_unit = lax.dynamic_slice_in_dim(unit_matrix, first_row, block_rows, 0)
    following = jnp.where(position + 1 < length, following, own_unit)
    return lax.all_gather(following, "state", axis=0, tiled=True)


def shards(anomalies, mean_state, obs_rows, obs_precision):
    current = anomalies
    window_count = anomalies.shape[0]
    members = anomalies.shape[2]
    unit_matrix = jnp.eye(members, dtype=jnp.float32)
    local_grams = gram_terms(current, mean_state, obs_rows, obs_precision)
    summed = lax.psum(local_grams, "state")
    transforms = [inverse_root(summed[0])]
    running = transforms[window_count - 1]
    later_product = rows_suffix(running, unit_matrix)
    current = jnp.stack([high_dot(current[0], high_dot(running, later_product))])
    return current


def solution(mesh):
    placed = (P("win", "state", None), P("win", "state"), P("win", "state"), P("win", "state"))
    return jax.shard_map(
        shards, mesh=mesh, in_specs=placed, out_specs=P("win", "state", None), check_vma=False
    )
```

profile of v0, /device:TPU:7, one launch (start us, length us, event | category | flops | bytes accessed | tf_op | source)
XLA Modules:
  0.0 101.5 jit_solution(14756415863204831308)
XLA Ops:
  6.5 0.7 copy-done.2
  7.9 0.6 copy-done.4
  8.6 1.2 %fusion.2 = f32[1,256,256]{2,1,0:T(8,128)} fusion(f32[128,256]{1,0:T(8,128)S(1)} %get-tuple-element.6, f32[128]{0:T(128)S(1)} %sqrt_bitcast_fusion, f32[128]{0:T(128)S(1)} %broadcast_multiply_fusion.1), kind=kOutput, calls=%fused_computation.6 | convolution fusion | flops 100794368 | bytes 394240 | tf_op jit(solution)/shard_map/wom,won->wmn/dot_general | solution.py:50
  9.8 20.3 %all-reduce.2.cloned.1.call-done = f32[1,256,256]{2,1,0:T(8,128)} async-done(((f32[1,256,256]{2,1,0:T(8,128)}), f32[1,256,256]{2,1,0:T(8,128)}) %all-reduce.2.cloned.1.call-update) | async-done | bytes 262160 | tf_op jit(solution)/shard_map/psum | solution.py:77
  30.1 1.7 %multiply_reduce_fusion = f32[]{:T(128)} fusion(f32[1,256,256]{2,1,0:T(8,128)} %all-reduce.2.cloned.1.call-done), kind=kLoop, calls=%fused_computation.29 | loop fusion | flops 327679 | bytes 262148 | tf_op jit(solution)/shard_map/reduce_sum | solution.py:26
  32.5 0.4 fusion.4
  34.6 1.0 select_reduce_fusion
  36.3 2.2 %collective-permute-start = (f32[128,256]{1,0:T(8,128)S(1)}, f32[128,256]{1,0:T(8,128)S(1)}, u32[]{:S(2)}, u32[]{:S(2)}) collective-permute-start(f32[128,256]{1,0:T(8,128)S(1)} %constant_dynamic-slice_fusion), channel_id=1, source_target_pairs={{2,0},{4,2},{6,4},{8,6},{10,8},{12,10},{14,12},{16,14},{18,16},{20... | collective-permute-start | bytes 393224 | tf_op jit(solution)/shard_map/ppermute | solution.py:15
  38.5 6.4 %collective-permute-done = f32[128,256]{1,0:T(8,128)S(1)} collective-permute-done((f32[128,256]{1,0:T(8,128)S(1)}, f32[128,256]{1,0:T(8,128)S(1)}, u32[]{:S(2)}, u32[]{:S(2)}) %collective-permute-start) | collective-permute-done | bytes 131104 | tf_op jit(solution)/shard_map/ppermute | solution.py:15
  44.9 2.6 %all_gather.15 = f32[256,256]{1,0:T(8,128)S(1)} all-gather(f32[128,256]{1,0:T(8,128)S(1)} %collective-permute-done), channel_id=1, replica_groups=mesh['win'=16,'state'=2] {'state'}, dimensions={0}, use_global_device_ids=true | all-gather | bytes 393216 | tf_op jit(solution)/shard_map/all_gather | solution.py:63
  47.8 1.9 %collective-permute-start.1 = (f32[128,256]{1,0:T(8,128)S(1)}, f32[128,256]{1,0:T(8,128)S(1)}, u32[]{:S(2)}, u32[]{:S(2)}) collective-permute-start(f32[128,256]{1,0:T(8,128)S(1)} %convolution_select_fusion.3), channel_id=1, source_target_pairs={{4,0},{6,2},{8,4},{10,6},{12,8},{14,10},{16,12},{18,14},{20,16},{2... | collective-permute-start | bytes 393224 | tf_op jit(solution)/shard_map/ppermute | solution.py:15
  49.8 5.6 %collective-permute-done.1 = f32[128,256]{1,0:T(8,128)S(1)} collective-permute-done((f32[128,256]{1,0:T(8,128)S(1)}, f32[128,256]{1,0:T(8,128)S(1)}, u32[]{:S(2)}, u32[]{:S(2)}) %collective-permute-start.1) | collective-permute-done | bytes 131104 | tf_op jit(solution)/shard_map/ppermute | solution.py:15
  55.3 2.8 %all_gather.16 = f32[256,256]{1,0:T(8,128)S(1)} all-gather(f32[128,256]{1,0:T(8,128)S(1)} %collective-permute-done.1), channel_id=1, replica_groups=mesh['win'=16,'state'=2] {'state'}, dimensions={0}, use_global_device_ids=true | all-gather | bytes 393216 | tf_op jit(solution)/shard_map/all_gather | solution.py:63
  58.4 1.3 %collective-permute-start.2 = (f32[128,256]{1,0:T(8,128)S(1)}, f32[128,256]{1,0:T(8,128)S(1)}, u32[]{:S(2)}, u32[]{:S(2)}) collective-permute-start(f32[128,256]{1,0:T(8,128)S(1)} %convolution_select_fusion.2), channel_id=1, source_target_pairs={{8,0},{10,2},{12,4},{14,6},{16,8},{18,10},{20,12},{22,14},{24,16},... | collective-permute-start | bytes 393224 | tf_op jit(solution)/shard_map/ppermute | solution.py:15
  59.8 5.3 %collective-permute-done.2 = f32[128,256]{1,0:T(8,128)S(1)} collective-permute-done((f32[128,256]{1,0:T(8,128)S(1)}, f32[128,256]{1,0:T(8,128)S(1)}, u32[]{:S(2)}, u32[]{:S(2)}) %collective-permute-start.2) | collective-permute-done | bytes 131104 | tf_op jit(solution)/shard_map/ppermute | solution.py:15
  65.1 2.8 %all_gather.17 = f32[256,256]{1,0:T(8,128)S(1)} all-gather(f32[128,256]{1,0:T(8,128)S(1)} %collective-permute-done.2), channel_id=1, replica_groups=mesh['win'=16,'state'=2] {'state'}, dimensions={0}, use_global_device_ids=true | all-gather | bytes 393216 | tf_op jit(solution)/shard_map/all_gather | solution.py:63
  68.2 1.3 %collective-permute-start.3 = (f32[128,256]{1,0:T(8,128)S(1)}, f32[128,256]{1,0:T(8,128)S(1)}, u32[]{:S(2)}, u32[]{:S(2)}) collective-permute-start(f32[128,256]{1,0:T(8,128)S(1)} %convolution_select_fusion.1), channel_id=1, source_target_pairs={{16,0},{18,2},{20,4},{22,6},{24,8},{26,10},{28,12},{30,14},{17,1},... | collective-permute-start | bytes 393224 | tf_op jit(solution)/shard_map/ppermute | solution.py:15
  69.5 9.0 %collective-permute-done.3 = f32[128,256]{1,0:T(8,128)S(1)} collective-permute-done((f32[128,256]{1,0:T(8,128)S(1)}, f32[128,256]{1,0:T(8,128)S(1)}, u32[]{:S(2)}, u32[]{:S(2)}) %collective-permute-start.3) | collective-permute-done | bytes 131104 | tf_op jit(solution)/shard_map/ppermute | solution.py:15
  78.5 2.8 %all_gather.18 = f32[256,256]{1,0:T(8,128)S(1)} all-gather(f32[128,256]{1,0:T(8,128)S(1)} %collective-permute-done.3), channel_id=1, replica_groups=mesh['win'=16,'state'=2] {'state'}, dimensions={0}, use_global_device_ids=true | all-gather | bytes 393216 | tf_op jit(solution)/shard_map/all_gather | solution.py:63
  81.6 1.9 %collective-permute-start.4 = (f32[128,256]{1,0:T(8,128)S(1)}, f32[128,256]{1,0:T(8,128)S(1)}, u32[]{:S(2)}, u32[]{:S(2)}) collective-permute-start(f32[128,256]{1,0:T(8,128)S(1)} %convolution_select_fusion), channel_id=1, source_target_pairs={{2,0},{4,2},{6,4},{8,6},{10,8},{12,10},{14,12},{16,14},{18,16},{20... | collective-permute-start | bytes 393224 | tf_op jit(solution)/shard_map/ppermute | solution.py:15
  83.5 6.5 %collective-permute-done.4 = f32[128,256]{1,0:T(8,128)S(1)} collective-permute-done((f32[128,256]{1,0:T(8,128)S(1)}, f32[128,256]{1,0:T(8,128)S(1)}, u32[]{:S(2)}, u32[]{:S(2)}) %collective-permute-start.4) | collective-permute-done | bytes 131104 | tf_op jit(solution)/shard_map/ppermute | solution.py:15
  90.0 2.8 %all_gather.19 = f32[256,256]{1,0:T(8,128)S(1)} all-gather(f32[128,256]{1,0:T(8,128)S(1)} %dynamic-slice_select_fusion), channel_id=1, replica_groups=mesh['win'=16,'state'=2] {'state'}, dimensions={0}, use_global_device_ids=true | all-gather | bytes 393216 | tf_op jit(solution)/shard_map/all_gather | solution.py:68
  93.2 0.6 convolution_bitcast_fusion
  93.8 0.8 copy.6
  (27 shorter events, 3.9 us)
Async XLA Ops:
  6.5 1.0 copy-start
  6.5 0.7 copy-start.2
  6.5 0.7 copy-start.3
  6.5 23.6 %all-reduce.2.cloned.1.call-start = ((), (), s32[]{:S(2)}) async-start(), calls=%async_computation | async-start | bytes 524288 | tf_op jit(solution)/shard_map/psum | solution.py:77
  7.9 0.7 copy-start.4
  30.1 2.4 %copy-start.1 = (f32[1,256,256]{2,1,0:T(8,128)S(1)}, f32[1,256,256]{2,1,0:T(8,128)}, u32[]{:S(2)}) copy-start(f32[1,256,256]{2,1,0:T(8,128)} %all-reduce.2.cloned.1.call-done) | copy-start | bytes 786436
  36.3 8.6 %collective-permute-start = (f32[128,256]{1,0:T(8,128)S(1)}, f32[128,256]{1,0:T(8,128)S(1)}, u32[]{:S(2)}, u32[]{:S(2)}) collective-permute-start(f32[128,256]{1,0:T(8,128)S(1)} %constant_dynamic-slice_fusion), channel_id=1, source_target_pairs={{2,0},{4,2},{6,4},{8,6},{10,8},{12,10},{14,12},{16,14},{18,16},{20... | collective-permute-start | bytes 393224 | tf_op jit(solution)/shard_map/ppermute | solution.py:15
  47.8 7.5 %collective-permute-start.1 = (f32[128,256]{1,0:T(8,128)S(1)}, f32[128,256]{1,0:T(8,128)S(1)}, u32[]{:S(2)}, u32[]{:S(2)}) collective-permute-start(f32[128,256]{1,0:T(8,128)S(1)} %convolution_select_fusion.3), channel_id=1, source_target_pairs={{4,0},{6,2},{8,4},{10,6},{12,8},{14,10},{16,12},{18,14},{20,16},{2... | collective-permute-start | bytes 393224 | tf_op jit(solution)/shard_map/ppermute | solution.py:15
  58.4 6.6 %collective-permute-start.2 = (f32[128,256]{1,0:T(8,128)S(1)}, f32[128,256]{1,0:T(8,128)S(1)}, u32[]{:S(2)}, u32[]{:S(2)}) collective-permute-start(f32[128,256]{1,0:T(8,128)S(1)} %convolution_select_fusion.2), channel_id=1, source_target_pairs={{8,0},{10,2},{12,4},{14,6},{16,8},{18,10},{20,12},{22,14},{24,16},... | collective-permute-start | bytes 393224 | tf_op jit(solution)/shard_map/ppermute | solution.py:15
  68.2 10.3 %collective-permute-start.3 = (f32[128,256]{1,0:T(8,128)S(1)}, f32[128,256]{1,0:T(8,128)S(1)}, u32[]{:S(2)}, u32[]{:S(2)}) collective-permute-start(f32[128,256]{1,0:T(8,128)S(1)} %convolution_select_fusion.1), channel_id=1, source_target_pairs={{16,0},{18,2},{20,4},{22,6},{24,8},{26,10},{28,12},{30,14},{17,1},... | collective-permute-start | bytes 393224 | tf_op jit(solution)/shard_map/ppermute | solution.py:15
  81.6 8.4 %collective-permute-start.4 = (f32[128,256]{1,0:T(8,128)S(1)}, f32[128,256]{1,0:T(8,128)S(1)}, u32[]{:S(2)}, u32[]{:S(2)}) collective-permute-start(f32[128,256]{1,0:T(8,128)S(1)} %convolution_select_fusion), channel_id=1, source_target_pairs={{2,0},{4,2},{6,4},{8,6},{10,8},{12,10},{14,12},{16,14},{18,16},{20... | collective-permute-start | bytes 393224 | tf_op jit(solution)/shard_map/ppermute | solution.py:15
Sparse Core Ops, SparseCore 0:
  9.9 20.1 all-reduce.1
where the time goes:
time: 102 us
  waiting for transfers between devices  53.1 us (52%)
  between operations  15 us (15%)
  blocking collectives  13.9 us (14%)
  starting transfers between devices  8.61 us (8%)
  matrix products  6.88 us (7%)
  local copies, waits for them, and re-layouts  2.29 us (2%)
  other arithmetic  1.75 us (2%)
    ppermute x5, waiting for transfers between devices, passed_along(): return lax.ppermute(x, axis, pairs)  32.8 us
    psum x1, waiting for transfers between devices, shards(): summed = lax.psum(local_grams, 'state')  20.3 us
    all_gather x4, blocking collectives, rows_suffix(): partner = lax.all_gather(received, 'state', axis=0, tiled=True)  11.1 us
    ppermute x5, starting transfers between devices, passed_along(): return lax.ppermute(x, axis, pairs)  8.61 us
    dot_general x12, matrix products, high_dot(): jnp.dot(left, right, precision=PRECISE, preferred_element_type=jnp.float32)  5.11 us
    all_gather x1, blocking collectives, rows_suffix(): return lax.all_gather(following, 'state', axis=0, tiled=True)  2.82 us
  transfers between devices with their start and end apart: 6, of which 6 were waited for; matrix products, arithmetic and copies ran while one was open for 0% of the time, Pallas kernels for 0%

commit v1 on v0

v1 whole, which is shorter than its diff:
```python
import functools

import jax
import jax.numpy as jnp
from jax import lax
from jax.experimental import pallas as pl
from jax.experimental.pallas import tpu as pltpu
from jax.sharding import PartitionSpec as P

NS_STEPS = 3
MESH = pl.DeviceIdType.MESH
F32 = jnp.float32
BF16 = jnp.bfloat16


def split2(x):
    hi = x.astype(BF16)
    return hi, (x - hi.astype(F32)).astype(BF16)


def mm(a, b):
    return jnp.dot(a, b, preferred_element_type=F32)


def dot3(a, b):
    (ah, al), (bh, bl) = a, b
    return mm(ah, bh) + (mm(ah, bl) + mm(al, bh))


def column(row, count):
    return jnp.transpose(jnp.broadcast_to(row, (8, count)))[:, :1]


def observed(x_ref, mean_ref, rows_ref, prec_ref):
    rows, members = x_ref.shape[1:]
    obs = rows_ref.shape[1]
    shifted = x_ref[0] + column(mean_ref[...], rows)
    wanted = column(rows_ref[...], obs)
    selector = (lax.broadcasted_iota(jnp.int32, (obs, rows), 1) == wanted).astype(BF16)
    hi = shifted.astype(BF16)
    rest = shifted - hi.astype(F32)
    mid = rest.astype(BF16)
    low = (rest - mid.astype(F32)).astype(BF16)
    predicted = jnp.tanh(mm(selector, hi) + mm(selector, mid) + mm(selector, low))
    centred = predicted - jnp.mean(predicted, axis=1, keepdims=True)
    return centred * jnp.sqrt(column(prec_ref[...], obs))


def gram_of(centred):
    left, right = split2(jnp.transpose(centred)), split2(centred)
    return dot3(left, right)


def inverse_root(gram):
    members = gram.shape[0]
    diagonal = lax.broadcasted_iota(jnp.int32, gram.shape, 0) == lax.broadcasted_iota(
        jnp.int32, gram.shape, 1
    )
    unit = diagonal.astype(F32)
    system = unit + gram
    root = system * (1.0 / jnp.sqrt(jnp.sum(system * system)))
    factor = 1.5 * unit - 0.5 * root
    inverse = split2(factor)
    root = split2(dot3(split2(root), inverse))
    full = None
    for step in range(1, NS_STEPS):
        factor = split2(1.5 * unit - 0.5 * dot3(inverse, root))
        if step + 1 < NS_STEPS:
            root = split2(dot3(root, factor))
        full = dot3(factor, inverse)
        inverse = split2(full)
    return full * (members / jnp.sum(jnp.where(diagonal, full, 0.0)))


def kernel(
    groups, size, parts, x_ref, mean_ref, rows_ref, prec_ref, out_ref,
    c_ref, t_ref, p_ref, v_ref,
    c_send, c_recv, t_send, t_recv, tf_send, tf_recv,
    z_send, z_recv, g_send, g_recv, gf_send, gf_recv,
):
    win, me = lax.axis_index("win"), lax.axis_index("state")
    z, k = win // size, lax.rem(win, size)
    members = x_ref.shape[2]
    share = members // parts
    block = members // (parts * size)

    def remote(ref, send, recv, device):
        return pltpu.make_async_remote_copy(
            src_ref=ref, dst_ref=ref, send_sem=send, recv_sem=recv,
            device_id=device, device_id_type=MESH,
        )

    def sibling(d):
        return win, lax.rem(me + d, parts)

    def peer(d):
        return z * size + lax.rem(k + d, size), me

    barrier = pltpu.get_barrier_semaphore()
    for d in range(1, parts):
        pl.semaphore_signal(barrier, inc=1, device_id=sibling(d), device_id_type=MESH)
    for d in range(1, size):
        pl.semaphore_signal(barrier, inc=1, device_id=peer(d), device_id_type=MESH)
    for d in range(1, groups):
        other = lax.rem(z + d, groups) * size + k
        pl.semaphore_signal(barrier, inc=1, device_id=(other, me), device_id_type=MESH)

    centred = observed(x_ref, mean_ref, rows_ref, prec_ref)
    c_ref[me] = centred
    pl.semaphore_wait(barrier, parts + size + groups - 3)

    sends = []
    for d in range(1, parts):
        copy = remote(c_ref.at[me], c_send.at[d], c_recv.at[me], sibling(d))
        copy.start()
        sends.append(copy)
    gram = gram_of(centred)
    for d in range(1, parts):
        src = lax.rem(me + parts - d, parts)
        remote(c_ref.at[src], c_send.at[d], c_recv.at[src], sibling(d)).wait_recv()
        gram = gram + gram_of(c_ref[src])
    transform = inverse_root(gram * (1.0 / (members - 1)))
    t_ref[k] = transform

    def t_rows(t, part):
        return t_ref.at[t, pl.ds(pl.multiple_of(part * share, share), share), :]

    for d in range(1, size):
        copy = remote(t_rows(k, me), t_send.at[d], t_recv.at[k], peer(d))
        copy.start()
        sends.append(copy)
    v_ref[...] = dot3(split2(x_ref[0]), split2(transform))
    for d in range(1, size):
        src = lax.rem(k + size - d, size)
        remote(t_rows(src, me), t_send.at[d], t_recv.at[src], peer(d)).wait_recv()
        for e in range(1, parts):
            copy = remote(t_rows(src, me), tf_send.at[d, e], tf_recv.at[src, me], sibling(e))
            copy.start()
            sends.append(copy)
    for d in range(1, size):
        src = lax.rem(k + size - d, size)
        for e in range(1, parts):
            part = lax.rem(me + parts - e, parts)
            remote(t_rows(src, part), tf_send.at[d, e], tf_recv.at[src, part], sibling(e)).wait_recv()

    def p_rows(group, index, part):
        first = (index * parts + part) * block
        return p_ref.at[group, pl.ds(pl.multiple_of(first, block), block), :]

    def to_group(d):
        return remote(p_rows(z, k, me), z_send.at[d], z_recv.at[z], ((z - d) * size + k, me))

    @pl.when(z > 0)
    def _():
        first = pl.multiple_of((k * parts + me) * block, block)
        rows = t_ref[0, pl.ds(first, block), :]
        for t in range(1, size):
            rows = dot3(split2(rows), split2(t_ref[t]))
        p_ref[z, pl.ds(first, block), :] = rows

    for d in range(1, groups):
        @pl.when(z >= d)
        def _():
            to_group(d).start()

    for t in range(1, size):
        @pl.when(t > k)
        def _():
            v_ref[...] = dot3(split2(v_ref[...]), split2(t_ref[t]))

    def to_peer(d, e):
        return remote(p_rows(z + d, k, me), g_send.at[d, e], g_recv.at[d, k], peer(e))

    def to_sibling(d, index, e):
        return remote(
            p_rows(z + d, index, me), gf_send.at[d, index, e], gf_recv.at[d, index, me], sibling(e)
        )

    for d in range(1, groups):
        @pl.when(z + d < groups)
        def _():
            remote(p_rows(z + d, k, me), z_send.at[d], z_recv.at[z + d], (win, me)).wait_recv()
            for e in range(1, size):
                to_peer(d, e).start()
            for e in range(1, parts):
                to_sibling(d, k, e).start()

    for d in range(1, groups):
        @pl.when(z + d < groups)
        def _():
            for e in range(1, size):
                src = lax.rem(k + size - e, size)
                remote(
                    p_rows(z + d, src, me), g_send.at[d, e], g_recv.at[d, src], peer(e)
                ).wait_recv()
                for f in range(1, parts):
                    to_sibling(d, src, f).start()

    for d in range(1, groups):
        @pl.when(z + d < groups)
        def _():
            for e in range(1, parts):
                part = lax.rem(me + parts - e, parts)
                for index in range(size):
                    remote(
                        p_rows(z + d, index, part), gf_send.at[d, index, e],
                        gf_recv.at[d, index, part], sibling(e),
                    ).wait_recv()
            v_ref[...] = dot3(split2(v_ref[...]), split2(p_ref[z + d]))

    out_ref[0] = v_ref[...]

    for copy in sends:
        copy.wait_send()
    for d in range(1, groups):
        @pl.when(z >= d)
        def _():
            to_group(d).wait_send()

        @pl.when(z + d < groups)
        def _():
            for e in range(1, size):
                to_peer(d, e).wait_send()
            for e in range(1, parts):
                for index in range(size):
                    to_sibling(d, index, e).wait_send()


def group_size(windows, parts, members):
    size = 1
    while size * size * 4 <= windows and windows % (size * 2) == 0 and members % (16 * size * parts) == 0:
        size *= 2
    return size


def solution(mesh):
    windows, parts = mesh.shape["win"], mesh.shape["state"]

    def shards(anomalies, mean_state, obs_rows, obs_precision):
        rows, members = anomalies.shape[1:]
        obs = obs_rows.shape[1]
        size = group_size(windows, parts, members)
        groups = windows // size
        dma = pltpu.SemaphoreType.DMA
        vmem = pl.BlockSpec(memory_space=pltpu.VMEM)
        return pl.pallas_call(
            functools.partial(kernel, groups, size, parts),
            out_shape=jax.ShapeDtypeStruct(anomalies.shape, F32),
            in_specs=[vmem] * 4,
            out_specs=vmem,
            scratch_shapes=[
                pltpu.VMEM((parts, obs, members), F32),
                pltpu.VMEM((size, members, members), F32),
                pltpu.VMEM((groups, members, members), F32),
                pltpu.VMEM((rows, members), F32),
                dma((parts,)), dma((parts,)),
                dma((size,)), dma((size,)),
                dma((size, parts)), dma((size, parts)),
                dma((groups,)), dma((groups,)),
                dma((groups, size)), dma((groups, size)),
                dma((groups, size, parts)), dma((groups, size, parts)),
            ],
            compiler_params=pltpu.CompilerParams(
                collective_id=0, has_side_effects=True, vmem_limit_bytes=48 * 1024 * 1024
            ),
        )(anomalies, mean_state, obs_rows, obs_precision)

    placed = (P("win", "state", None), P("win", "state"), P("win", "state"), P("win", "state"))
    return jax.shard_map(
        shards, mesh=mesh, in_specs=placed, out_specs=P("win", "state", None), check_vma=False
    )
```

time: 102 us -> 33.2 us (0.33)
  the two profiles are of different devices: /device:TPU:7 before, /device:TPU:1 now
where the time goes in v1:
time: 33.2 us; the launch traced here: 33 us
  Pallas kernels  29.3 us (88%)
  local copies, waits for them, and re-layouts  3.64 us (11%)
    pallas_call x1, Pallas kernels, shards(): pl.pallas_call(functools.partial(kernel, groups, size, parts), out_shape=...  29.3 us
    unnamed x9, local copies, waits for them, and re-layouts  3.64 us

profile of v1, /device:TPU:1, one launch (start us, length us, event | category | flops | bytes accessed | tf_op | source)
XLA Modules:
  0.0 33.0 jit_solution(16417178863688784728)
XLA Ops:
  0.0 0.0 copy-start
  0.0 0.9 %copy-done = f32[1,256,256]{2,1,0:T(8,128)S(1)} copy-done((f32[1,256,256]{2,1,0:T(8,128)S(1)}, f32[1,256,256]{2,1,0:T(8,128)}, u32[]{:S(2)}) %copy-start) | copy-done | bytes 262168
  1.0 0.0 copy-start.1
  1.0 0.7 %copy-done.1 = f32[1,256]{1,0:T(1,128)S(1)} copy-done((f32[1,256]{1,0:T(1,128)S(1)}, f32[1,256]{1,0:T(1,128)}, u32[]{:S(2)}) %copy-start.1) | copy-done | bytes 1048
  1.6 0.0 copy-start.2
  1.6 0.7 %copy-done.2 = s32[1,128]{1,0:T(1,128)S(1)} copy-done((s32[1,128]{1,0:T(1,128)S(1)}, s32[1,128]{1,0:T(1,128)}, u32[]{:S(2)}) %copy-start.2) | copy-done | bytes 536
  2.3 0.0 copy-start.3
  2.3 0.7 %copy-done.3 = f32[1,128]{1,0:T(1,128)S(1)} copy-done((f32[1,128]{1,0:T(1,128)S(1)}, f32[1,128]{1,0:T(1,128)}, u32[]{:S(2)}) %copy-start.3) | copy-done | bytes 536
  2.9 29.3 %shard_map.46 = f32[1,256,256]{2,1,0:T(8,128)S(1)} custom-call(f32[1,256,256]{2,1,0:T(8,128)S(1)} %copy-done, f32[1,256]{1,0:T(1,128)S(1)} %copy-done.1, s32[1,128]{1,0:T(1,128)S(1)} %copy-done.2, f32[1,128]{1,0:T(1,128)S(1)} %copy-done.3), custom_call_target="tpu_custom_call" | custom-call | tf_op jit(solution)/shard_map/pallas_call | solution.py:246
  32.3 0.7 %copy.6 = f32[1,256,256]{2,1,0:T(8,128)} copy(f32[1,256,256]{2,1,0:T(8,128)S(1)} %shard_map.46) | data formatting | bytes 524288
Async XLA Ops:
  0.0 0.9 %copy-start = (f32[1,256,256]{2,1,0:T(8,128)S(1)}, f32[1,256,256]{2,1,0:T(8,128)}, u32[]{:S(2)}) copy-start(f32[1,256,256]{2,1,0:T(8,128)} %x_ref.1) | copy-start | bytes 786436
  1.0 0.7 %copy-start.1 = (f32[1,256]{1,0:T(1,128)S(1)}, f32[1,256]{1,0:T(1,128)}, u32[]{:S(2)}) copy-start(f32[1,256]{1,0:T(1,128)} %mean_ref.1) | copy-start | bytes 3076
  1.6 0.7 %copy-start.2 = (s32[1,128]{1,0:T(1,128)S(1)}, s32[1,128]{1,0:T(1,128)}, u32[]{:S(2)}) copy-start(s32[1,128]{1,0:T(1,128)} %rows_ref.1) | copy-start | bytes 1540
  2.3 0.7 %copy-start.3 = (f32[1,128]{1,0:T(1,128)S(1)}, f32[1,128]{1,0:T(1,128)}, u32[]{:S(2)}) copy-start(f32[1,128]{1,0:T(1,128)} %prec_ref.1) | copy-start | bytes 1540

commit v2 on v1

--- a/solution.py
+++ b/solution.py
@@ -24,7 +24,7 @@
 
 def dot3(a, b):
     (ah, al), (bh, bl) = a, b
-    return mm(ah, bh) + (mm(ah, bl) + mm(al, bh))
+    return mm(jnp.concatenate([ah, ah, al], axis=1), jnp.concatenate([bh, bl, bh], axis=0))
 
 
 def column(row, count):
@@ -32,9 +32,9 @@
 
 
 def observed(x_ref, mean_ref, rows_ref, prec_ref):
-    rows, members = x_ref.shape[1:]
+    rows, members = x_ref.shape
     obs = rows_ref.shape[1]
-    shifted = x_ref[0] + column(mean_ref[...], rows)
+    shifted = x_ref[...] + column(mean_ref[...], rows)
     wanted = column(rows_ref[...], obs)
     selector = (lax.broadcasted_iota(jnp.int32, (obs, rows), 1) == wanted).astype(BF16)
     hi = shifted.astype(BF16)
@@ -73,14 +73,22 @@
 
 
 def kernel(
-    groups, size, parts, x_ref, mean_ref, rows_ref, prec_ref, out_ref,
-    c_ref, t_ref, p_ref, v_ref,
+    groups, size, parts, x_hbm, mean_hbm, rows_hbm, prec_hbm, out_ref,
+    x_ref, mean_ref, rows_ref, prec_ref, in_sem, c_ref, t_ref, p_ref, v_ref,
     c_send, c_recv, t_send, t_recv, tf_send, tf_recv,
     z_send, z_recv, g_send, g_recv, gf_send, gf_recv,
 ):
     win, me = lax.axis_index("win"), lax.axis_index("state")
     z, k = win // size, lax.rem(win, size)
-    members = x_ref.shape[2]
+    fetches = [
+        pltpu.make_async_copy(src, dst, in_sem.at[i])
+        for i, (src, dst) in enumerate(
+            [(mean_hbm, mean_ref), (rows_hbm, rows_ref), (prec_hbm, prec_ref), (x_hbm.at[0], x_ref)]
+        )
+    ]
+    for fetch in fetches:
+        fetch.start()
+    members = x_ref.shape[1]
     share = members // parts
     block = members // (parts * size)
 
@@ -105,6 +113,8 @@
         other = lax.rem(z + d, groups) * size + k
         pl.semaphore_signal(barrier, inc=1, device_id=(other, me), device_id_type=MESH)
 
+    for fetch in fetches:
+        fetch.wait()
     centred = observed(x_ref, mean_ref, rows_ref, prec_ref)
     c_ref[me] = centred
     pl.semaphore_wait(barrier, parts + size + groups - 3)
@@ -129,7 +139,7 @@
         copy = remote(t_rows(k, me), t_send.at[d], t_recv.at[k], peer(d))
         copy.start()
         sends.append(copy)
-    v_ref[...] = dot3(split2(x_ref[0]), split2(transform))
+    v_ref[...] = dot3(split2(x_ref[...]), split2(transform))
     for d in range(1, size):
         src = lax.rem(k + size - d, size)
         remote(t_rows(src, me), t_send.at[d], t_recv.at[src], peer(d)).wait_recv()
@@ -246,9 +256,14 @@
         return pl.pallas_call(
             functools.partial(kernel, groups, size, parts),
             out_shape=jax.ShapeDtypeStruct(anomalies.shape, F32),
-            in_specs=[vmem] * 4,
+            in_specs=[pl.BlockSpec(memory_space=pl.ANY)] * 4,
             out_specs=vmem,
             scratch_shapes=[
+                pltpu.VMEM((rows, members), F32),
+                pltpu.VMEM((1, rows), F32),
+                pltpu.VMEM((1, obs), jnp.int32),
+                pltpu.VMEM((1, obs), F32),
+                dma((4,)),
                 pltpu.VMEM((parts, obs, members), F32),
                 pltpu.VMEM((size, members, members), F32),
                 pltpu.VMEM((groups, members, members), F32),
@@ -261,7 +276,7 @@
                 dma((groups, size, parts)), dma((groups, size, parts)),
             ],
             compiler_params=pltpu.CompilerParams(
-                collective_id=0, has_side_effects=True, vmem_limit_bytes=48 * 1024 * 1024
+                collective_id=0, has_side_effects=True, vmem_limit_bytes=56 * 1024 * 1024
             ),
         )(anomalies, mean_state, obs_rows, obs_precision)
 

time: 33.2 us -> 31.9 us (0.961)
  local copies, waits for them, and re-layouts: 3.64 us -> 1.67 us
  Pallas kernels: 29.3 us -> 30.1 us
    unnamed x9 -> x1, local copies, waits for them, and re-layouts: 3.64 us -> 1.67 us
    pallas_call x1, Pallas kernels: 29.3 us -> 30.1 us  [shards(): pl.pallas_call(functools.partial(kernel, groups, size, parts), out_shape=...]
where the time goes in v2:
time: 31.9 us; the launch traced here: 31.8 us
  Pallas kernels  30.1 us (94%)
  local copies, waits for them, and re-layouts  1.67 us (5%)
    pallas_call x1, Pallas kernels, shards(): pl.pallas_call(functools.partial(kernel, groups, size, parts), out_shape=...  30.1 us
    unnamed x1, local copies, waits for them, and re-layouts  1.67 us

profile of v2, /device:TPU:1, one launch (start us, length us, event | category | flops | bytes accessed | tf_op | source)
XLA Modules:
  0.0 31.8 jit_solution(17350487682311829777)
XLA Ops:
  0.0 30.1 %shard_map.46 = f32[1,256,256]{2,1,0:T(8,128)} custom-call(f32[1,256,256]{2,1,0:T(8,128)} %x_hbm.1, f32[1,256]{1,0:T(1,128)} %mean_hbm.1, s32[1,128]{1,0:T(1,128)} %rows_hbm.1, f32[1,128]{1,0:T(1,128)} %prec_hbm.1), custom_call_target="tpu_custom_call" | custom-call | tf_op jit(solution)/shard_map/pallas_call | solution.py:256
  30.1 1.7 %copy.6 = f32[1,256,256]{2,1,0:T(8,128)} copy(f32[1,256,256]{2,1,0:T(8,128)} %shard_map.46) | data formatting | bytes 524288

commit v3 on v2

--- a/solution.py
+++ b/solution.py
@@ -72,9 +72,57 @@
     return full * (members / jnp.sum(jnp.where(diagonal, full, 0.0)))
 
 
+def flipped(index, bits):
+    result, bit = index, 1
+    while bit <= bits:
+        if bits & bit:
+            result = result + bit * (1 - 2 * lax.rem(index // bit, 2))
+        bit *= 2
+    return result
+
+
+def positions(half):
+    return (
+        lax.broadcasted_iota(jnp.int32, (half, half), 0),
+        lax.broadcasted_iota(jnp.int32, (half, half), 1),
+    )
+
+
+def pack(matrix, ref, slot):
+    half, parts, share = matrix.shape[0] // 2, ref.shape[1], ref.shape[2] - 8
+    r, c = positions(half)
+    upper, lower = matrix[:half, :half], matrix[half:, half:]
+    both = jnp.where(r <= c, upper, lower)
+    diagonal = jnp.sum(jnp.where(r == c, lower, 0.0), axis=0, keepdims=True)
+    tail = jnp.broadcast_to(jnp.concatenate([diagonal, diagonal], axis=1), (8, 2 * half))
+    for part in range(parts):
+        rows = slice(part * share, (part + 1) * share)
+        ref[slot, part, :share, :half] = both[rows]
+        ref[slot, part, :share, half:] = matrix[rows, half:]
+        ref[slot, part, share:, :] = tail
+
+
+def unpacked(ref, slot):
+    parts, share, half = ref.shape[1], ref.shape[2] - 8, ref.shape[3] // 2
+    r, c = positions(half)
+    rows = jnp.concatenate([ref[slot, part, :share, :] for part in range(parts)], axis=0)
+    both, right = rows[:, :half], rows[:, half:]
+    turned = jnp.transpose(both)
+    diagonal = ref[slot, 0, share : share + 1, :half]
+    upper = jnp.where(r <= c, both, turned)
+    lower = jnp.where(r > c, both, jnp.where(r == c, diagonal, turned))
+    return jnp.concatenate(
+        [
+            jnp.concatenate([upper, right], axis=1),
+            jnp.concatenate([jnp.transpose(right), lower], axis=1),
+        ],
+        axis=0,
+    )
+
+
 def kernel(
     groups, size, parts, x_hbm, mean_hbm, rows_hbm, prec_hbm, out_ref,
-    x_ref, mean_ref, rows_ref, prec_ref, in_sem, c_ref, t_ref, p_ref, v_ref,
+    x_ref, mean_ref, rows_ref, prec_ref, in_sem, c_ref, tp_ref, t_ref, th_ref, tl_ref, p_ref, v_ref,
     c_send, c_recv, t_send, t_recv, tf_send, tf_recv,
     z_send, z_recv, g_send, g_recv, gf_send, gf_recv,
 ):
@@ -89,7 +137,6 @@
     for fetch in fetches:
         fetch.start()
     members = x_ref.shape[1]
-    share = members // parts
     block = members // (parts * size)
 
     def remote(ref, send, recv, device):
@@ -102,7 +149,7 @@
         return win, lax.rem(me + d, parts)
 
     def peer(d):
-        return z * size + lax.rem(k + d, size), me
+        return z * size + flipped(k, d), me
 
     barrier = pltpu.get_barrier_semaphore()
     for d in range(1, parts):
@@ -130,43 +177,47 @@
         remote(c_ref.at[src], c_send.at[d], c_recv.at[src], sibling(d)).wait_recv()
         gram = gram + gram_of(c_ref[src])
     transform = inverse_root(gram * (1.0 / (members - 1)))
-    t_ref[k] = transform
-
-    def t_rows(t, part):
-        return t_ref.at[t, pl.ds(pl.multiple_of(part * share, share), share), :]
+    pack(transform, tp_ref, k)
+
+    def t_share(t, part):
+        return tp_ref.at[t, part]
 
     for d in range(1, size):
-        copy = remote(t_rows(k, me), t_send.at[d], t_recv.at[k], peer(d))
+        copy = remote(t_share(k, me), t_send.at[d], t_recv.at[d], peer(d))
         copy.start()
         sends.append(copy)
-    v_ref[...] = dot3(split2(x_ref[...]), split2(transform))
+    own = split2(transform)
+    t_ref[k], th_ref[k], tl_ref[k] = transform, own[0], own[1]
+    v_ref[...] = dot3(split2(x_ref[...]), own)
     for d in range(1, size):
-        src = lax.rem(k + size - d, size)
-        remote(t_rows(src, me), t_send.at[d], t_recv.at[src], peer(d)).wait_recv()
+        src = flipped(k, d)
+        remote(t_share(src, me), t_send.at[d], t_recv.at[d], peer(d)).wait_recv()
         for e in range(1, parts):
-            copy = remote(t_rows(src, me), tf_send.at[d, e], tf_recv.at[src, me], sibling(e))
+            copy = remote(t_share(src, me), tf_send.at[d, e], tf_recv.at[d, me], sibling(e))
             copy.start()
             sends.append(copy)
     for d in range(1, size):
-        src = lax.rem(k + size - d, size)
+        src = flipped(k, d)
         for e in range(1, parts):
             part = lax.rem(me + parts - e, parts)
-            remote(t_rows(src, part), tf_send.at[d, e], tf_recv.at[src, part], sibling(e)).wait_recv()
-
-    def p_rows(group, index, part):
-        first = (index * parts + part) * block
-        return p_ref.at[group, pl.ds(pl.multiple_of(first, block), block), :]
+            remote(t_share(src, part), tf_send.at[d, e], tf_recv.at[d, part], sibling(e)).wait_recv()
+        received = unpacked(tp_ref, src)
+        t_ref[src] = received
+        th_ref[src], tl_ref[src] = split2(received)
+
+    def p_rows(group, index):
+        return p_ref.at[group, me, pl.ds(pl.multiple_of(index * block, block), block), :]
 
     def to_group(d):
-        return remote(p_rows(z, k, me), z_send.at[d], z_recv.at[z], ((z - d) * size + k, me))
+        return remote(p_rows(z, k), z_send.at[d], z_recv.at[d], ((z - d) * size + k, me))
 
     @pl.when(z > 0)
     def _():
-        first = pl.multiple_of((k * parts + me) * block, block)
+        first = pl.multiple_of((me * size + k) * block, block)
         rows = t_ref[0, pl.ds(first, block), :]
         for t in range(1, size):
-            rows = dot3(split2(rows), split2(t_ref[t]))
-        p_ref[z, pl.ds(first, block), :] = rows
+            rows = dot3(split2(rows), (th_ref[t], tl_ref[t]))
+        p_ref[z, me, pl.ds(pl.multiple_of(k * block, block), block), :] = rows
 
     for d in range(1, groups):
         @pl.when(z >= d)
@@ -176,47 +227,44 @@
     for t in range(1, size):
         @pl.when(t > k)
         def _():
-            v_ref[...] = dot3(split2(v_ref[...]), split2(t_ref[t]))
+            v_ref[...] = dot3(split2(v_ref[...]), (th_ref[t], tl_ref[t]))
 
     def to_peer(d, e):
-        return remote(p_rows(z + d, k, me), g_send.at[d, e], g_recv.at[d, k], peer(e))
-
-    def to_sibling(d, index, e):
-        return remote(
-            p_rows(z + d, index, me), gf_send.at[d, index, e], gf_recv.at[d, index, me], sibling(e)
-        )
+        return remote(p_rows(z + d, k), g_send.at[d, e], g_recv.at[d, e], peer(e))
+
+    def to_sibling(d, e):
+        return remote(p_ref.at[z + d, me], gf_send.at[d, e], gf_recv.at[d, me], sibling(e))
+
+    def finish(d):
+        for e in range(1, parts):
+            part = lax.rem(me + parts - e, parts)
+            remote(
+                p_ref.at[z + d, part], gf_send.at[d, e], gf_recv.at[d, part], sibling(e)
+            ).wait_recv()
+        product = jnp.concatenate([p_ref[z + d, part] for part in range(parts)], axis=0)
+        v_ref[...] = dot3(split2(v_ref[...]), split2(product))
 
     for d in range(1, groups):
         @pl.when(z + d < groups)
         def _():
-            remote(p_rows(z + d, k, me), z_send.at[d], z_recv.at[z + d], (win, me)).wait_recv()
+            remote(p_rows(z + d, k), z_send.at[d], z_recv.at[d], (win, me)).wait_recv()
             for e in range(1, size):
                 to_peer(d, e).start()
+
+    for d in range(1, groups):
+        @pl.when(z + d < groups)
+        def _():
+            for e in range(1, size):
+                src = flipped(k, e)
+                remote(p_rows(z + d, src), g_send.at[d, e], g_recv.at[d, e], peer(e)).wait_recv()
             for e in range(1, parts):
-                to_sibling(d, k, e).start()
-
-    for d in range(1, groups):
-        @pl.when(z + d < groups)
-        def _():
-            for e in range(1, size):
-                src = lax.rem(k + size - e, size)
-                remote(
-                    p_rows(z + d, src, me), g_send.at[d, e], g_recv.at[d, src], peer(e)
-                ).wait_recv()
-                for f in range(1, parts):
-                    to_sibling(d, src, f).start()
-
-    for d in range(1, groups):
-        @pl.when(z + d < groups)
-        def _():
-            for e in range(1, parts):
-                part = lax.rem(me + parts - e, parts)
-                for index in range(size):
-                    remote(
-                        p_rows(z + d, index, part), gf_send.at[d, index, e],
-                        gf_recv.at[d, index, part], sibling(e),
-                    ).wait_recv()
-            v_ref[...] = dot3(split2(v_ref[...]), split2(p_ref[z + d]))
+                to_sibling(d, e).start()
+            if d > 1:
+                finish(d - 1)
+
+        @pl.when(z + d == groups - 1)
+        def _():
+            finish(d)
 
     out_ref[0] = v_ref[...]
 
@@ -232,8 +280,7 @@
             for e in range(1, size):
                 to_peer(d, e).wait_send()
             for e in range(1, parts):
-                for index in range(size):
-                    to_sibling(d, index, e).wait_send()
+                to_sibling(d, e).wait_send()
 
 
 def group_size(windows, parts, members):
@@ -256,7 +303,7 @@
         return pl.pallas_call(
             functools.partial(kernel, groups, size, parts),
             out_shape=jax.ShapeDtypeStruct(anomalies.shape, F32),
-            in_specs=[pl.BlockSpec(memory_space=pl.ANY)] * 4,
+            in_specs=[pl.BlockSpec(memory_space=pltpu.HBM)] * 4,
             out_specs=vmem,
             scratch_shapes=[
                 pltpu.VMEM((rows, members), F32),
@@ -265,15 +312,18 @@
                 pltpu.VMEM((1, obs), F32),
                 dma((4,)),
                 pltpu.VMEM((parts, obs, members), F32),
+                pltpu.VMEM((size, parts, members // (2 * parts) + 8, members), F32),
                 pltpu.VMEM((size, members, members), F32),
-                pltpu.VMEM((groups, members, members), F32),
+                pltpu.VMEM((size, members, members), BF16),
+                pltpu.VMEM((size, members, members), BF16),
+                pltpu.VMEM((groups, parts, members // parts, members), F32),
                 pltpu.VMEM((rows, members), F32),
                 dma((parts,)), dma((parts,)),
                 dma((size,)), dma((size,)),
                 dma((size, parts)), dma((size, parts)),
                 dma((groups,)), dma((groups,)),
                 dma((groups, size)), dma((groups, size)),
-                dma((groups, size, parts)), dma((groups, size, parts)),
+                dma((groups, parts)), dma((groups, parts)),
             ],
             compiler_params=pltpu.CompilerParams(
                 collective_id=0, has_side_effects=True, vmem_limit_bytes=56 * 1024 * 1024

time: 31.9 us -> 29.4 us (0.922)
  Pallas kernels: 30.1 us -> 27.5 us
    pallas_call x1, Pallas kernels: 30.1 us -> 27.5 us  [shards(): pl.pallas_call(functools.partial(kernel, groups, size, parts), out_shape=...]
where the time goes in v3:
time: 29.4 us; the launch traced here: 29.2 us
  Pallas kernels  27.5 us (94%)
  local copies, waits for them, and re-layouts  1.67 us (6%)
    pallas_call x1, Pallas kernels, shards(): pl.pallas_call(functools.partial(kernel, groups, size, parts), out_shape=...  27.5 us
    unnamed x1, local copies, waits for them, and re-layouts  1.67 us

profile of v3, /device:TPU:1, one launch (start us, length us, event | category | flops | bytes accessed | tf_op | source)
XLA Modules:
  0.0 29.2 jit_solution(6934101419279239880)
XLA Ops:
  0.0 27.5 %shard_map.46 = f32[1,256,256]{2,1,0:T(8,128)} custom-call(f32[1,256,256]{2,1,0:T(8,128)} %x_hbm.1, f32[1,256]{1,0:T(1,128)} %mean_hbm.1, s32[1,128]{1,0:T(1,128)} %rows_hbm.1, f32[1,128]{1,0:T(1,128)} %prec_hbm.1), custom_call_target="tpu_custom_call" | custom-call | tf_op jit(solution)/shard_map/pallas_call | solution.py:303
  27.5 1.7 %copy.6 = f32[1,256,256]{2,1,0:T(8,128)} copy(f32[1,256,256]{2,1,0:T(8,128)} %shard_map.46) | data formatting | bytes 524288

commit v4 on v3

--- a/solution.py
+++ b/solution.py
@@ -152,19 +152,22 @@
         return z * size + flipped(k, d), me
 
     barrier = pltpu.get_barrier_semaphore()
-    for d in range(1, parts):
-        pl.semaphore_signal(barrier, inc=1, device_id=sibling(d), device_id_type=MESH)
-    for d in range(1, size):
-        pl.semaphore_signal(barrier, inc=1, device_id=peer(d), device_id_type=MESH)
-    for d in range(1, groups):
-        other = lax.rem(z + d, groups) * size + k
-        pl.semaphore_signal(barrier, inc=1, device_id=(other, me), device_id_type=MESH)
+    for e in range(1, parts):
+        pl.semaphore_signal(barrier, inc=1, device_id=sibling(e), device_id_type=MESH)
+    for e in range(parts):
+        part = lax.rem(me + e, parts)
+        for d in range(1, size):
+            device = (z * size + flipped(k, d), part)
+            pl.semaphore_signal(barrier, inc=1, device_id=device, device_id_type=MESH)
+        for d in range(1, groups):
+            device = (lax.rem(z + d, groups) * size + k, part)
+            pl.semaphore_signal(barrier, inc=1, device_id=device, device_id_type=MESH)
 
     for fetch in fetches:
         fetch.wait()
     centred = observed(x_ref, mean_ref, rows_ref, prec_ref)
     c_ref[me] = centred
-    pl.semaphore_wait(barrier, parts + size + groups - 3)
+    pl.semaphore_wait(barrier, parts - 1 + parts * (size + groups - 2))
 
     sends = []
     for d in range(1, parts):
@@ -179,50 +182,77 @@
     transform = inverse_root(gram * (1.0 / (members - 1)))
     pack(transform, tp_ref, k)
 
-    def t_share(t, part):
-        return tp_ref.at[t, part]
+    def to_lead(d, part):
+        return remote(
+            tp_ref.at[k, part], t_send.at[d], t_recv.at[d, part], (z * size + flipped(k, d), 0)
+        )
+
+    def from_lead(d, e):
+        return remote(
+            tp_ref.at[flipped(k, d)], tf_send.at[d, e], tf_recv.at[d], (win, e)
+        )
+
+    def keep(d):
+        src = flipped(k, d)
+        received = unpacked(tp_ref, src)
+        t_ref[src] = received
+        th_ref[src], tl_ref[src] = split2(received)
 
     for d in range(1, size):
-        copy = remote(t_share(k, me), t_send.at[d], t_recv.at[d], peer(d))
+        copy = to_lead(d, me)
         copy.start()
         sends.append(copy)
     own = split2(transform)
     t_ref[k], th_ref[k], tl_ref[k] = transform, own[0], own[1]
     v_ref[...] = dot3(split2(x_ref[...]), own)
-    for d in range(1, size):
-        src = flipped(k, d)
-        remote(t_share(src, me), t_send.at[d], t_recv.at[d], peer(d)).wait_recv()
-        for e in range(1, parts):
-            copy = remote(t_share(src, me), tf_send.at[d, e], tf_recv.at[d, me], sibling(e))
-            copy.start()
-            sends.append(copy)
-    for d in range(1, size):
-        src = flipped(k, d)
-        for e in range(1, parts):
-            part = lax.rem(me + parts - e, parts)
-            remote(t_share(src, part), tf_send.at[d, e], tf_recv.at[d, part], sibling(e)).wait_recv()
-        received = unpacked(tp_ref, src)
-        t_ref[src] = received
-        th_ref[src], tl_ref[src] = split2(received)
-
-    def p_rows(group, index):
-        return p_ref.at[group, me, pl.ds(pl.multiple_of(index * block, block), block), :]
-
-    def to_group(d):
-        return remote(p_rows(z, k), z_send.at[d], z_recv.at[d], ((z - d) * size + k, me))
-
-    @pl.when(z > 0)
+
+    def p_rows(group, part, index):
+        return p_ref.at[group, part, pl.ds(pl.multiple_of(index * block, block), block), :]
+
+    def to_group(d, part):
+        return remote(
+            p_rows(z, part, k), z_send.at[d, part], z_recv.at[d], ((z - d) * size + k, part)
+        )
+
+    @pl.when(me == 0)
     def _():
-        first = pl.multiple_of((me * size + k) * block, block)
-        rows = t_ref[0, pl.ds(first, block), :]
-        for t in range(1, size):
-            rows = dot3(split2(rows), (th_ref[t], tl_ref[t]))
-        p_ref[z, me, pl.ds(pl.multiple_of(k * block, block), block), :] = rows
-
-    for d in range(1, groups):
-        @pl.when(z >= d)
+        for d in range(1, size):
+            src = flipped(k, d)
+            for part in range(parts):
+                remote(
+                    tp_ref.at[src, part], t_send.at[d], t_recv.at[d, part], (win, me)
+                ).wait_recv()
+            for e in range(1, parts):
+                from_lead(d, e).start()
+            keep(d)
+
+        @pl.when(z > 0)
         def _():
-            to_group(d).start()
+            rows = jnp.concatenate(
+                [
+                    t_ref[0, pl.ds(pl.multiple_of((part * size + k) * block, block), block), :]
+                    for part in range(parts)
+                ],
+                axis=0,
+            )
+            for t in range(1, size):
+                rows = dot3(split2(rows), (th_ref[t], tl_ref[t]))
+            for part in range(parts):
+                p_ref[z, part, pl.ds(pl.multiple_of(k * block, block), block), :] = rows[
+                    part * block : (part + 1) * block
+                ]
+
+        for d in reversed(range(1, groups)):
+            @pl.when(z >= d)
+            def _():
+                for part in range(parts):
+                    to_group(d, part).start()
+
+    @pl.when(me > 0)
+    def _():
+        for d in range(1, size):
+            remote(tp_ref.at[flipped(k, d)], t_send.at[d], tf_recv.at[d], (win, me)).wait_recv()
+            keep(d)
 
     for t in range(1, size):
         @pl.when(t > k)
@@ -230,10 +260,23 @@
             v_ref[...] = dot3(split2(v_ref[...]), (th_ref[t], tl_ref[t]))
 
     def to_peer(d, e):
-        return remote(p_rows(z + d, k), g_send.at[d, e], g_recv.at[d, e], peer(e))
+        return remote(p_rows(z + d, me, k), g_send.at[d, e], g_recv.at[d, e], peer(e))
 
     def to_sibling(d, e):
         return remote(p_ref.at[z + d, me], gf_send.at[d, e], gf_recv.at[d, me], sibling(e))
+
+    def spread(d):
+        remote(p_rows(z + d, me, k), z_send.at[d, 0], z_recv.at[d], (win, me)).wait_recv()
+        for e in reversed(range(1, size)):
+            to_peer(d, e).start()
+
+    def share(d):
+        for e in range(1, size):
+            remote(
+                p_rows(z + d, me, flipped(k, e)), g_send.at[d, e], g_recv.at[d, e], peer(e)
+            ).wait_recv()
+        for e in range(1, parts):
+            to_sibling(d, e).start()
 
     def finish(d):
         for e in range(1, parts):
@@ -244,37 +287,28 @@
         product = jnp.concatenate([p_ref[z + d, part] for part in range(parts)], axis=0)
         v_ref[...] = dot3(split2(v_ref[...]), split2(product))
 
-    for d in range(1, groups):
-        @pl.when(z + d < groups)
-        def _():
-            remote(p_rows(z + d, k), z_send.at[d], z_recv.at[d], (win, me)).wait_recv()
-            for e in range(1, size):
-                to_peer(d, e).start()
-
-    for d in range(1, groups):
-        @pl.when(z + d < groups)
-        def _():
-            for e in range(1, size):
-                src = flipped(k, e)
-                remote(p_rows(z + d, src), g_send.at[d, e], g_recv.at[d, e], peer(e)).wait_recv()
-            for e in range(1, parts):
-                to_sibling(d, e).start()
-            if d > 1:
-                finish(d - 1)
-
-        @pl.when(z + d == groups - 1)
-        def _():
-            finish(d)
+    for step in range(1, groups + 2):
+        for late, stage in enumerate((spread, share, finish)):
+            if 1 <= step - late < groups:
+                pl.when(z + step - late < groups)(functools.partial(stage, step - late))
 
     out_ref[0] = v_ref[...]
 
     for copy in sends:
         copy.wait_send()
+
+    @pl.when(me == 0)
+    def _():
+        for d in range(1, size):
+            for e in range(1, parts):
+                from_lead(d, e).wait_send()
+        for d in range(1, groups):
+            @pl.when(z >= d)
+            def _():
+                for part in range(parts):
+                    to_group(d, part).wait_send()
+
     for d in range(1, groups):
-        @pl.when(z >= d)
-        def _():
-            to_group(d).wait_send()
-
         @pl.when(z + d < groups)
         def _():
             for e in range(1, size):
@@ -302,7 +336,7 @@
         vmem = pl.BlockSpec(memory_space=pltpu.VMEM)
         return pl.pallas_call(
             functools.partial(kernel, groups, size, parts),
-            out_shape=jax.ShapeDtypeStruct(anomalies.shape, F32),
+            out_shape=pltpu.VMEM(anomalies.shape, F32),
             in_specs=[pl.BlockSpec(memory_space=pltpu.HBM)] * 4,
             out_specs=vmem,
             scratch_shapes=[
@@ -319,9 +353,9 @@
                 pltpu.VMEM((groups, parts, members // parts, members), F32),
                 pltpu.VMEM((rows, members), F32),
                 dma((parts,)), dma((parts,)),
-                dma((size,)), dma((size,)),
-                dma((size, parts)), dma((size, parts)),
-                dma((groups,)), dma((groups,)),
+                dma((size,)), dma((size, parts)),
+                dma((size, parts)), dma((size,)),
+                dma((groups, parts)), dma((groups,)),
                 dma((groups, size)), dma((groups, size)),
                 dma((groups, parts)), dma((groups, parts)),
             ],

time: 29.4 us -> 29.7 us (1.010)
  Pallas kernels: 27.5 us -> 28.7 us
  local copies, waits for them, and re-layouts: 1.67 us -> 0.71 us
    pallas_call x1, Pallas kernels: 27.5 us -> 28.7 us  [shards(): pl.pallas_call(functools.partial(kernel, groups, size, parts), out_shape=...]
    unnamed x1, local copies, waits for them, and re-layouts: 1.67 us -> 0.71 us
where the time goes in v4:
time: 29.7 us; the launch traced here: 29.5 us
  Pallas kernels  28.7 us (97%)
  local copies, waits for them, and re-layouts  0.71 us (2%)
    pallas_call x1, Pallas kernels, shards(): pl.pallas_call(functools.partial(kernel, groups, size, parts), out_shape=...  28.7 us
    unnamed x1, local copies, waits for them, and re-layouts  0.71 us

profile of v4, /device:TPU:1, one launch (start us, length us, event | category | flops | bytes accessed | tf_op | source)
XLA Modules:
  0.0 29.5 jit_solution(977193907537419932)
XLA Ops:
  0.0 28.7 %shard_map.46 = f32[1,256,256]{2,1,0:T(8,128)S(1)} custom-call(f32[1,256,256]{2,1,0:T(8,128)} %x_hbm.1, f32[1,256]{1,0:T(1,128)} %mean_hbm.1, s32[1,128]{1,0:T(1,128)} %rows_hbm.1, f32[1,128]{1,0:T(1,128)} %prec_hbm.1), custom_call_target="tpu_custom_call" | custom-call | tf_op jit(solution)/shard_map/pallas_call | solution.py:337
  28.8 0.7 %copy.6 = f32[1,256,256]{2,1,0:T(8,128)} copy(f32[1,256,256]{2,1,0:T(8,128)S(1)} %shard_map.46) | data formatting | bytes 524288

commit v5 on v4

--- a/solution.py
+++ b/solution.py
@@ -124,7 +124,7 @@
     groups, size, parts, x_hbm, mean_hbm, rows_hbm, prec_hbm, out_ref,
     x_ref, mean_ref, rows_ref, prec_ref, in_sem, c_ref, tp_ref, t_ref, th_ref, tl_ref, p_ref, v_ref,
     c_send, c_recv, t_send, t_recv, tf_send, tf_recv,
-    z_send, z_recv, g_send, g_recv, gf_send, gf_recv,
+    z_send, z_recv, zf_send, zf_recv, g_send, g_recv, gf_send, gf_recv,
 ):
     win, me = lax.axis_index("win"), lax.axis_index("state")
     z, k = win // size, lax.rem(win, size)
@@ -214,6 +214,11 @@
             p_rows(z, part, k), z_send.at[d, part], z_recv.at[d], ((z - d) * size + k, part)
         )
 
+    far = flipped(k, size - 1)
+
+    def to_first(part):
+        return remote(p_rows(z, part, far), zf_send.at[part], zf_recv.at[z], (k, part))
+
     @pl.when(me == 0)
     def _():
         for d in range(1, size):
@@ -226,11 +231,10 @@
                 from_lead(d, e).start()
             keep(d)
 
-        @pl.when(z > 0)
-        def _():
+        def make_rows(index):
             rows = jnp.concatenate(
                 [
-                    t_ref[0, pl.ds(pl.multiple_of((part * size + k) * block, block), block), :]
+                    t_ref[0, pl.ds(pl.multiple_of((part * size + index) * block, block), block), :]
                     for part in range(parts)
                 ],
                 axis=0,
@@ -238,16 +242,23 @@
             for t in range(1, size):
                 rows = dot3(split2(rows), (th_ref[t], tl_ref[t]))
             for part in range(parts):
-                p_ref[z, part, pl.ds(pl.multiple_of(k * block, block), block), :] = rows[
+                p_ref[z, part, pl.ds(pl.multiple_of(index * block, block), block), :] = rows[
                     part * block : (part + 1) * block
                 ]
 
+        pl.when(z > 0)(lambda: make_rows(k))
         for d in reversed(range(1, groups)):
             @pl.when(z >= d)
             def _():
                 for part in range(parts):
                     to_group(d, part).start()
 
+        @pl.when(jnp.logical_and(z > 0, z < groups - 1))
+        def _():
+            make_rows(far)
+            for part in range(parts):
+                to_first(part).start()
+
     @pl.when(me > 0)
     def _():
         for d in range(1, size):
@@ -265,16 +276,33 @@
     def to_sibling(d, e):
         return remote(p_ref.at[z + d, me], gf_send.at[d, e], gf_recv.at[d, me], sibling(e))
 
+    def far_peer(d, act):
+        if d == groups - 1:
+            act()
+        else:
+            pl.when(z > 0)(act)
+
     def spread(d):
         remote(p_rows(z + d, me, k), z_send.at[d, 0], z_recv.at[d], (win, me)).wait_recv()
-        for e in reversed(range(1, size)):
+        far_peer(d, lambda: to_peer(d, size - 1).start())
+        for e in range(1, size - 1):
             to_peer(d, e).start()
 
+    def from_peer(d, e):
+        remote(
+            p_rows(z + d, me, flipped(k, e)), g_send.at[d, e], g_recv.at[d, e], peer(e)
+        ).wait_recv()
+
     def share(d):
-        for e in range(1, size):
-            remote(
-                p_rows(z + d, me, flipped(k, e)), g_send.at[d, e], g_recv.at[d, e], peer(e)
-            ).wait_recv()
+        for e in range(1, size - 1):
+            from_peer(d, e)
+        far_peer(d, lambda: from_peer(d, size - 1))
+        if d < groups - 1:
+            @pl.when(z == 0)
+            def _():
+                remote(
+                    p_rows(d, me, far), zf_send.at[0], zf_recv.at[d], (win, me)
+                ).wait_recv()
         for e in range(1, parts):
             to_sibling(d, e).start()
 
@@ -308,11 +336,17 @@
                 for part in range(parts):
                     to_group(d, part).wait_send()
 
+        @pl.when(jnp.logical_and(z > 0, z < groups - 1))
+        def _():
+            for part in range(parts):
+                to_first(part).wait_send()
+
     for d in range(1, groups):
         @pl.when(z + d < groups)
         def _():
-            for e in range(1, size):
+            for e in range(1, size - 1):
                 to_peer(d, e).wait_send()
+            far_peer(d, lambda: to_peer(d, size - 1).wait_send())
             for e in range(1, parts):
                 to_sibling(d, e).wait_send()
 
@@ -355,7 +389,7 @@
                 dma((parts,)), dma((parts,)),
                 dma((size,)), dma((size, parts)),
                 dma((size, parts)), dma((size,)),
-                dma((groups, parts)), dma((groups,)),
+                dma((groups, parts)), dma((groups,)), dma((parts,)), dma((groups,)),
                 dma((groups, size)), dma((groups, size)),
                 dma((groups, parts)), dma((groups, parts)),
             ],

time: 29.7 us -> 29 us (0.976)
  Pallas kernels: 28.7 us -> 28.1 us
    pallas_call x1, Pallas kernels: 28.7 us -> 28.1 us  [shards(): pl.pallas_call(functools.partial(kernel, groups, size, parts), out_shape=...]
where the time goes in v5:
time: 29 us; the launch traced here: 28.8 us
  Pallas kernels  28.1 us (97%)
  local copies, waits for them, and re-layouts  0.71 us (2%)
    pallas_call x1, Pallas kernels, shards(): pl.pallas_call(functools.partial(kernel, groups, size, parts), out_shape=...  28.1 us
    unnamed x1, local copies, waits for them, and re-layouts  0.71 us

profile of v5, /device:TPU:1, one launch (start us, length us, event | category | flops | bytes accessed | tf_op | source)
XLA Modules:
  0.0 28.8 jit_solution(16737542076123386197)
XLA Ops:
  0.0 28.1 %shard_map.46 = f32[1,256,256]{2,1,0:T(8,128)S(1)} custom-call(f32[1,256,256]{2,1,0:T(8,128)} %x_hbm.1, f32[1,256]{1,0:T(1,128)} %mean_hbm.1, s32[1,128]{1,0:T(1,128)} %rows_hbm.1, f32[1,128]{1,0:T(1,128)} %prec_hbm.1), custom_call_target="tpu_custom_call" | custom-call | tf_op jit(solution)/shard_map/pallas_call | solution.py:371
  28.1 0.7 %copy.6 = f32[1,256,256]{2,1,0:T(8,128)} copy(f32[1,256,256]{2,1,0:T(8,128)S(1)} %shard_map.46) | data formatting | bytes 524288

commit v6 on v5

--- a/solution.py
+++ b/solution.py
@@ -24,7 +24,17 @@
 
 def dot3(a, b):
     (ah, al), (bh, bl) = a, b
-    return mm(jnp.concatenate([ah, ah, al], axis=1), jnp.concatenate([bh, bl, bh], axis=0))
+    right = jnp.concatenate([bh, bl, bh], axis=0)
+    half = ah.shape[0] // 2
+    if half % 128:
+        return mm(jnp.concatenate([ah, ah, al], axis=1), right)
+    return jnp.concatenate(
+        [
+            mm(jnp.concatenate([h, h, l], axis=1), right)
+            for h, l in ((ah[:half], al[:half]), (ah[half:], al[half:]))
+        ],
+        axis=0,
+    )
 
 
 def column(row, count):

time: 29 us -> 28.8 us (level)
  no operation moved by 1% of the time
where the time goes in v6:
time: 28.8 us; the launch traced here: 28.6 us
  Pallas kernels  27.9 us (97%)
  local copies, waits for them, and re-layouts  0.71 us (2%)
    pallas_call x1, Pallas kernels, shards(): pl.pallas_call(functools.partial(kernel, groups, size, parts), out_shape=...  27.9 us
    unnamed x1, local copies, waits for them, and re-layouts  0.71 us

profile of v6, /device:TPU:1, one launch (start us, length us, event | category | flops | bytes accessed | tf_op | source)
XLA Modules:
  0.0 28.6 jit_solution(7910429334453385020)
XLA Ops:
  0.0 27.9 %shard_map.46 = f32[1,256,256]{2,1,0:T(8,128)S(1)} custom-call(f32[1,256,256]{2,1,0:T(8,128)} %x_hbm.1, f32[1,256]{1,0:T(1,128)} %mean_hbm.1, s32[1,128]{1,0:T(1,128)} %rows_hbm.1, f32[1,128]{1,0:T(1,128)} %prec_hbm.1), custom_call_target="tpu_custom_call" | custom-call | tf_op jit(solution)/shard_map/pallas_call | solution.py:381
  27.9 0.7 %copy.6 = f32[1,256,256]{2,1,0:T(8,128)} copy(f32[1,256,256]{2,1,0:T(8,128)S(1)} %shard_map.46) | data formatting | bytes 524288

commit v7 on v4

--- a/solution.py
+++ b/solution.py
@@ -102,13 +102,13 @@
         ref[slot, part, share:, :] = tail
 
 
-def unpacked(ref, slot):
-    parts, share, half = ref.shape[1], ref.shape[2] - 8, ref.shape[3] // 2
+def unpacked(shares):
+    share, half = shares[0].shape[0] - 8, shares[0].shape[1] // 2
     r, c = positions(half)
-    rows = jnp.concatenate([ref[slot, part, :share, :] for part in range(parts)], axis=0)
+    rows = jnp.concatenate([part[:share] for part in shares], axis=0)
     both, right = rows[:, :half], rows[:, half:]
     turned = jnp.transpose(both)
-    diagonal = ref[slot, 0, share : share + 1, :half]
+    diagonal = shares[0][share : share + 1, :half]
     upper = jnp.where(r <= c, both, turned)
     lower = jnp.where(r > c, both, jnp.where(r == c, diagonal, turned))
     return jnp.concatenate(
@@ -122,7 +122,7 @@
 
 def kernel(
     groups, size, parts, x_hbm, mean_hbm, rows_hbm, prec_hbm, out_ref,
-    x_ref, mean_ref, rows_ref, prec_ref, in_sem, c_ref, tp_ref, t_ref, th_ref, tl_ref, p_ref, v_ref,
+    x_ref, mean_ref, rows_ref, prec_ref, in_sem, c_ref, tp_ref, t_ref, th_ref, tl_ref, q_ref, p_ref, v_ref,
     c_send, c_recv, t_send, t_recv, tf_send, tf_recv,
     z_send, z_recv, g_send, g_recv, gf_send, gf_recv,
 ):
@@ -194,20 +194,68 @@
 
     def keep(d):
         src = flipped(k, d)
-        received = unpacked(tp_ref, src)
+        received = unpacked([tp_ref[src, part] for part in range(parts)])
         t_ref[src] = received
         th_ref[src], tl_ref[src] = split2(received)
+
+    def whole(d, part):
+        return q_ref.at[part] if d == 1 else p_ref.at[z + d, part]
+
+    def piece(d, index):
+        return q_ref.at[me, index] if d == 1 else p_rows(z + d, me, index)
+
+    def p_rows(group, part, index):
+        return p_ref.at[group, part, pl.ds(pl.multiple_of(index * block, block), block), :]
+
+    def to_previous():
+        return pltpu.make_async_remote_copy(
+            src_ref=tp_ref.at[k, me], dst_ref=q_ref.at[me, k], send_sem=z_send.at[1, 0],
+            recv_sem=z_recv.at[1], device_id=((z - 1) * size + k, me), device_id_type=MESH,
+        )
+
+    def to_peer(d, e):
+        return remote(piece(d, k), g_send.at[d, e], g_recv.at[d, e], peer(e))
+
+    def to_sibling(d, e):
+        return remote(whole(d, me), gf_send.at[d, e], gf_recv.at[d, me], sibling(e))
+
+    def spread(d):
+        remote(piece(d, k), z_send.at[d, 0], z_recv.at[d], (win, me)).wait_recv()
+        for e in range(1, size):
+            to_peer(d, e).start()
+
+    def share(d):
+        for e in range(1, size):
+            remote(piece(d, flipped(k, e)), g_send.at[d, e], g_recv.at[d, e], peer(e)).wait_recv()
+        for e in range(1, parts):
+            to_sibling(d, e).start()
+
+    def finish(d):
+        for e in range(1, parts):
+            part = lax.rem(me + parts - e, parts)
+            remote(
+                whole(d, part), gf_send.at[d, e], gf_recv.at[d, part], sibling(e)
+            ).wait_recv()
+        if d == 1:
+            for t in range(size):
+                later = unpacked([q_ref[part, t] for part in range(parts)])
+                v_ref[...] = dot3(split2(v_ref[...]), split2(later))
+        else:
+            product = jnp.concatenate([p_ref[z + d, part] for part in range(parts)], axis=0)
+            v_ref[...] = dot3(split2(v_ref[...]), split2(product))
 
     for d in range(1, size):
         copy = to_lead(d, me)
         copy.start()
         sends.append(copy)
+
+    @pl.when(z > 0)
+    def _():
+        to_previous().start()
+
     own = split2(transform)
     t_ref[k], th_ref[k], tl_ref[k] = transform, own[0], own[1]
     v_ref[...] = dot3(split2(x_ref[...]), own)
-
-    def p_rows(group, part, index):
-        return p_ref.at[group, part, pl.ds(pl.multiple_of(index * block, block), block), :]
 
     def to_group(d, part):
         return remote(
@@ -218,6 +266,8 @@
     def _():
         for d in range(1, size):
             src = flipped(k, d)
+            if d == size - 1:
+                pl.when(z + 1 < groups)(functools.partial(spread, 1))
             for part in range(parts):
                 remote(
                     tp_ref.at[src, part], t_send.at[d], t_recv.at[d, part], (win, me)
@@ -226,7 +276,7 @@
                 from_lead(d, e).start()
             keep(d)
 
-        @pl.when(z > 0)
+        @pl.when(z > 1)
         def _():
             rows = jnp.concatenate(
                 [
@@ -242,7 +292,7 @@
                     part * block : (part + 1) * block
                 ]
 
-        for d in reversed(range(1, groups)):
+        for d in reversed(range(2, groups)):
             @pl.when(z >= d)
             def _():
                 for part in range(parts):
@@ -251,6 +301,8 @@
     @pl.when(me > 0)
     def _():
         for d in range(1, size):
+            if d == size - 1:
+                pl.when(z + 1 < groups)(functools.partial(spread, 1))
             remote(tp_ref.at[flipped(k, d)], t_send.at[d], tf_recv.at[d], (win, me)).wait_recv()
             keep(d)
 
@@ -259,38 +311,15 @@
         def _():
             v_ref[...] = dot3(split2(v_ref[...]), (th_ref[t], tl_ref[t]))
 
-    def to_peer(d, e):
-        return remote(p_rows(z + d, me, k), g_send.at[d, e], g_recv.at[d, e], peer(e))
-
-    def to_sibling(d, e):
-        return remote(p_ref.at[z + d, me], gf_send.at[d, e], gf_recv.at[d, me], sibling(e))
-
-    def spread(d):
-        remote(p_rows(z + d, me, k), z_send.at[d, 0], z_recv.at[d], (win, me)).wait_recv()
-        for e in reversed(range(1, size)):
-            to_peer(d, e).start()
-
-    def share(d):
-        for e in range(1, size):
-            remote(
-                p_rows(z + d, me, flipped(k, e)), g_send.at[d, e], g_recv.at[d, e], peer(e)
-            ).wait_recv()
-        for e in range(1, parts):
-            to_sibling(d, e).start()
-
-    def finish(d):
-        for e in range(1, parts):
-            part = lax.rem(me + parts - e, parts)
-            remote(
-                p_ref.at[z + d, part], gf_send.at[d, e], gf_recv.at[d, part], sibling(e)
-            ).wait_recv()
-        product = jnp.concatenate([p_ref[z + d, part] for part in range(parts)], axis=0)
-        v_ref[...] = dot3(split2(v_ref[...]), split2(product))
-
-    for step in range(1, groups + 2):
-        for late, stage in enumerate((spread, share, finish)):
-            if 1 <= step - late < groups:
-                pl.when(z + step - late < groups)(functools.partial(stage, step - late))
+    pl.when(z + 1 < groups)(functools.partial(share, 1))
+    for d in range(2, groups):
+        pl.when(z + d < groups)(functools.partial(spread, d))
+    for d in range(1, groups):
+        if d > 1:
+            pl.when(z + d < groups)(functools.partial(share, d))
+            pl.when(z + d - 1 < groups)(functools.partial(finish, d - 1))
+        if d == groups - 1:
+            pl.when(z + d < groups)(functools.partial(finish, d))
 
     out_ref[0] = v_ref[...]
 
@@ -302,11 +331,15 @@
         for d in range(1, size):
             for e in range(1, parts):
                 from_lead(d, e).wait_send()
-        for d in range(1, groups):
+        for d in range(2, groups):
             @pl.when(z >= d)
             def _():
                 for part in range(parts):
                     to_group(d, part).wait_send()
+
+    @pl.when(z > 0)
+    def _():
+        to_previous().wait_send()
 
     for d in range(1, groups):
         @pl.when(z + d < groups)
@@ -350,6 +383,7 @@
                 pltpu.VMEM((size, members, members), F32),
                 pltpu.VMEM((size, members, members), BF16),
                 pltpu.VMEM((size, members, members), BF16),
+                pltpu.VMEM((parts, size, members // (2 * parts) + 8, members), F32),
                 pltpu.VMEM((groups, parts, members // parts, members), F32),
                 pltpu.VMEM((rows, members), F32),
                 dma((parts,)), dma((parts,)),

time: 29.7 us -> 27.5 us (0.926)
  Pallas kernels: 28.7 us -> 26.6 us
    pallas_call x1, Pallas kernels: 28.7 us -> 26.6 us  [shards(): pl.pallas_call(functools.partial(kernel, groups, size, parts), out_shape=...]
where the time goes in v7:
time: 27.5 us; the launch traced here: 27.3 us
  Pallas kernels  26.6 us (97%)
  local copies, waits for them, and re-layouts  0.71 us (3%)
    pallas_call x1, Pallas kernels, shards(): pl.pallas_call(functools.partial(kernel, groups, size, parts), out_shape=...  26.6 us
    unnamed x1, local copies, waits for them, and re-layouts  0.71 us

profile of v7, /device:TPU:1, one launch (start us, length us, event | category | flops | bytes accessed | tf_op | source)
XLA Modules:
  0.0 27.3 jit_solution(17153927487067537877)
XLA Ops:
  0.0 26.6 %shard_map.46 = f32[1,256,256]{2,1,0:T(8,128)S(1)} custom-call(f32[1,256,256]{2,1,0:T(8,128)} %x_hbm.1, f32[1,256]{1,0:T(1,128)} %mean_hbm.1, s32[1,128]{1,0:T(1,128)} %rows_hbm.1, f32[1,128]{1,0:T(1,128)} %prec_hbm.1), custom_call_target="tpu_custom_call" | custom-call | tf_op jit(solution)/shard_map/pallas_call | solution.py:370
  26.6 0.7 %copy.6 = f32[1,256,256]{2,1,0:T(8,128)} copy(f32[1,256,256]{2,1,0:T(8,128)S(1)} %shard_map.46) | data formatting | bytes 524288

commit v8 on v7

--- a/solution.py
+++ b/solution.py
@@ -182,9 +182,19 @@
     transform = inverse_root(gram * (1.0 / (members - 1)))
     pack(transform, tp_ref, k)
 
-    def to_lead(d, part):
+    share_rows = tp_ref.shape[2] - 8
+
+    def packed(ref, first, second, part):
+        return ref.at[first, second] if part == 0 else ref.at[first, second, pl.ds(0, share_rows), :]
+
+    def by_part(act):
+        pl.when(me == 0)(lambda: act(0))
+        pl.when(me > 0)(lambda: act(1))
+
+    def to_lead(d, kind):
         return remote(
-            tp_ref.at[k, part], t_send.at[d], t_recv.at[d, part], (z * size + flipped(k, d), 0)
+            packed(tp_ref, k, me, kind), t_send.at[d], t_recv.at[d, me],
+            (z * size + flipped(k, d), 0),
         )
 
     def from_lead(d, e):
@@ -201,32 +211,46 @@
     def whole(d, part):
         return q_ref.at[part] if d == 1 else p_ref.at[z + d, part]
 
-    def piece(d, index):
-        return q_ref.at[me, index] if d == 1 else p_rows(z + d, me, index)
+    def piece(d, index, kind):
+        return packed(q_ref, me, index, kind) if d == 1 else p_rows(z + d, me, index)
+
+    def pieces(d, act):
+        if d == 1:
+            by_part(act)
+        else:
+            act(0)
 
     def p_rows(group, part, index):
         return p_ref.at[group, part, pl.ds(pl.multiple_of(index * block, block), block), :]
 
-    def to_previous():
+    def to_previous(kind):
         return pltpu.make_async_remote_copy(
-            src_ref=tp_ref.at[k, me], dst_ref=q_ref.at[me, k], send_sem=z_send.at[1, 0],
+            src_ref=packed(tp_ref, k, me, kind), dst_ref=packed(q_ref, me, k, kind), send_sem=z_send.at[1, 0],
             recv_sem=z_recv.at[1], device_id=((z - 1) * size + k, me), device_id_type=MESH,
         )
 
-    def to_peer(d, e):
-        return remote(piece(d, k), g_send.at[d, e], g_recv.at[d, e], peer(e))
+    def to_peer(d, e, kind):
+        return remote(piece(d, k, kind), g_send.at[d, e], g_recv.at[d, e], peer(e))
 
     def to_sibling(d, e):
         return remote(whole(d, me), gf_send.at[d, e], gf_recv.at[d, me], sibling(e))
 
     def spread(d):
-        remote(piece(d, k), z_send.at[d, 0], z_recv.at[d], (win, me)).wait_recv()
-        for e in range(1, size):
-            to_peer(d, e).start()
+        def act(kind):
+            remote(piece(d, k, kind), z_send.at[d, 0], z_recv.at[d], (win, me)).wait_recv()
+            for e in range(1, size):
+                to_peer(d, e, kind).start()
+
+        pieces(d, act)
 
     def share(d):
-        for e in range(1, size):
-            remote(piece(d, flipped(k, e)), g_send.at[d, e], g_recv.at[d, e], peer(e)).wait_recv()
+        def act(kind):
+            for e in range(1, size):
+                remote(
+                    piece(d, flipped(k, e), kind), g_send.at[d, e], g_recv.at[d, e], peer(e)
+                ).wait_recv()
+
+        pieces(d, act)
         for e in range(1, parts):
             to_sibling(d, e).start()
 
@@ -244,14 +268,12 @@
             product = jnp.concatenate([p_ref[z + d, part] for part in range(parts)], axis=0)
             v_ref[...] = dot3(split2(v_ref[...]), split2(product))
 
-    for d in range(1, size):
-        copy = to_lead(d, me)
-        copy.start()
-        sends.append(copy)
-
-    @pl.when(z > 0)
-    def _():
-        to_previous().start()
+    def send_own(kind):
+        for d in range(1, size):
+            to_lead(d, kind).start()
+        pl.when(z > 0)(lambda: to_previous(kind).start())
+
+    by_part(send_own)
 
     own = split2(transform)
     t_ref[k], th_ref[k], tl_ref[k] = transform, own[0], own[1]
@@ -270,7 +292,7 @@
                 pl.when(z + 1 < groups)(functools.partial(spread, 1))
             for part in range(parts):
                 remote(
-                    tp_ref.at[src, part], t_send.at[d], t_recv.at[d, part], (win, me)
+                    packed(tp_ref, src, part, part), t_send.at[d], t_recv.at[d, part], (win, me)
                 ).wait_recv()
             for e in range(1, parts):
                 from_lead(d, e).start()
@@ -314,9 +336,10 @@
     pl.when(z + 1 < groups)(functools.partial(share, 1))
     for d in range(2, groups):
         pl.when(z + d < groups)(functools.partial(spread, d))
-    for d in range(1, groups):
-        if d > 1:
-            pl.when(z + d < groups)(functools.partial(share, d))
+    pl.when(z + 1 < groups)(functools.partial(finish, 1))
+    for d in range(2, groups):
+        pl.when(z + d < groups)(functools.partial(share, d))
+        if d > 2:
             pl.when(z + d - 1 < groups)(functools.partial(finish, d - 1))
         if d == groups - 1:
             pl.when(z + d < groups)(functools.partial(finish, d))
@@ -337,15 +360,21 @@
                 for part in range(parts):
                     to_group(d, part).wait_send()
 
-    @pl.when(z > 0)
-    def _():
-        to_previous().wait_send()
+    def own_sent(kind):
+        for d in range(1, size):
+            to_lead(d, kind).wait_send()
+        pl.when(z > 0)(lambda: to_previous(kind).wait_send())
+
+    by_part(own_sent)
 
     for d in range(1, groups):
         @pl.when(z + d < groups)
         def _():
-            for e in range(1, size):
-                to_peer(d, e).wait_send()
+            def sent(kind):
+                for e in range(1, size):
+                    to_peer(d, e, kind).wait_send()
+
+            pieces(d, sent)
             for e in range(1, parts):
                 to_sibling(d, e).wait_send()
 

time: 27.5 us -> 27.3 us (level)
  no operation moved by 1% of the time
where the time goes in v8:
time: 27.3 us; the launch traced here: 27.2 us
  Pallas kernels  26.5 us (97%)
  local copies, waits for them, and re-layouts  0.71 us (3%)
    pallas_call x1, Pallas kernels, shards(): pl.pallas_call(functools.partial(kernel, groups, size, parts), out_shape=...  26.5 us
    unnamed x1, local copies, waits for them, and re-layouts  0.71 us

profile of v8, /device:TPU:1, one launch (start us, length us, event | category | flops | bytes accessed | tf_op | source)
XLA Modules:
  0.0 27.2 jit_solution(18114943464456664974)
XLA Ops:
  0.0 26.5 %shard_map.46 = f32[1,256,256]{2,1,0:T(8,128)S(1)} custom-call(f32[1,256,256]{2,1,0:T(8,128)} %x_hbm.1, f32[1,256]{1,0:T(1,128)} %mean_hbm.1, s32[1,128]{1,0:T(1,128)} %rows_hbm.1, f32[1,128]{1,0:T(1,128)} %prec_hbm.1), custom_call_target="tpu_custom_call" | custom-call | tf_op jit(solution)/shard_map/pallas_call | solution.py:399
  26.5 0.7 %copy.6 = f32[1,256,256]{2,1,0:T(8,128)} copy(f32[1,256,256]{2,1,0:T(8,128)S(1)} %shard_map.46) | data formatting | bytes 524288

commit v9 on v8

--- a/solution.py
+++ b/solution.py
@@ -58,18 +58,22 @@
     )
     unit = diagonal.astype(F32)
     system = unit + gram
-    root = system * (1.0 / jnp.sqrt(jnp.sum(system * system)))
-    factor = 1.5 * unit - 0.5 * root
-    inverse = split2(factor)
-    root = split2(dot3(split2(root), inverse))
-    full = None
+    scale = 1.0 / jnp.sqrt(jnp.sum(system * system))
+    parted = split2(system)
+    square = dot3(parted, parted)
+    full = 1.5 * unit - (0.5 * scale) * system
+    root = split2((1.5 * scale) * system - (0.5 * scale * scale) * square)
+    inverse = split2(full)
+    trace = jnp.sum(jnp.where(diagonal, full, 0.0))
     for step in range(1, NS_STEPS):
-        factor = split2(1.5 * unit - 0.5 * dot3(inverse, root))
+        wide = 1.5 * unit - 0.5 * dot3(inverse, root)
+        factor = split2(wide)
         if step + 1 < NS_STEPS:
             root = split2(dot3(root, factor))
+        trace = jnp.sum(wide * full)
         full = dot3(factor, inverse)
         inverse = split2(full)
-    return full * (members / jnp.sum(jnp.where(diagonal, full, 0.0)))
+    return full * (members / trace)
 
 
 def flipped(index, bits):
@@ -124,7 +128,7 @@
     groups, size, parts, x_hbm, mean_hbm, rows_hbm, prec_hbm, out_ref,
     x_ref, mean_ref, rows_ref, prec_ref, in_sem, c_ref, tp_ref, t_ref, th_ref, tl_ref, q_ref, p_ref, v_ref,
     c_send, c_recv, t_send, t_recv, tf_send, tf_recv,
-    z_send, z_recv, g_send, g_recv, gf_send, gf_recv,
+    z_send, z_recv, zf_send, zf_recv, g_send, g_recv, gf_send, gf_recv,
 ):
     win, me = lax.axis_index("win"), lax.axis_index("state")
     z, k = win // size, lax.rem(win, size)
@@ -235,20 +239,27 @@
     def to_sibling(d, e):
         return remote(whole(d, me), gf_send.at[d, e], gf_recv.at[d, me], sibling(e))
 
+    far = flipped(k, size - 1)
+
+    def near(d):
+        return range(1, size - 1 if d == groups - 1 else size)
+
     def spread(d):
         def act(kind):
             remote(piece(d, k, kind), z_send.at[d, 0], z_recv.at[d], (win, me)).wait_recv()
-            for e in range(1, size):
+            for e in near(d):
                 to_peer(d, e, kind).start()
 
         pieces(d, act)
 
     def share(d):
         def act(kind):
-            for e in range(1, size):
+            for e in near(d):
                 remote(
                     piece(d, flipped(k, e), kind), g_send.at[d, e], g_recv.at[d, e], peer(e)
                 ).wait_recv()
+            if d == groups - 1:
+                remote(piece(d, far, kind), zf_send.at[0], zf_recv.at[0], (win, me)).wait_recv()
 
         pieces(d, act)
         for e in range(1, parts):
@@ -284,6 +295,9 @@
             p_rows(z, part, k), z_send.at[d, part], z_recv.at[d], ((z - d) * size + k, part)
         )
 
+    def to_first(part):
+        return remote(p_rows(z, part, far), zf_send.at[part], zf_recv.at[0], (k, part))
+
     @pl.when(me == 0)
     def _():
         for d in range(1, size):
@@ -298,11 +312,10 @@
                 from_lead(d, e).start()
             keep(d)
 
-        @pl.when(z > 1)
-        def _():
+        def make_rows(index):
             rows = jnp.concatenate(
                 [
-                    t_ref[0, pl.ds(pl.multiple_of((part * size + k) * block, block), block), :]
+                    t_ref[0, pl.ds(pl.multiple_of((part * size + index) * block, block), block), :]
                     for part in range(parts)
                 ],
                 axis=0,
@@ -310,15 +323,22 @@
             for t in range(1, size):
                 rows = dot3(split2(rows), (th_ref[t], tl_ref[t]))
             for part in range(parts):
-                p_ref[z, part, pl.ds(pl.multiple_of(k * block, block), block), :] = rows[
+                p_ref[z, part, pl.ds(pl.multiple_of(index * block, block), block), :] = rows[
                     part * block : (part + 1) * block
                 ]
 
+        pl.when(z > 1)(lambda: make_rows(k))
         for d in reversed(range(2, groups)):
             @pl.when(z >= d)
             def _():
                 for part in range(parts):
                     to_group(d, part).start()
+
+        @pl.when(z == groups - 1)
+        def _():
+            make_rows(far)
+            for part in range(parts):
+                to_first(part).start()
 
     @pl.when(me > 0)
     def _():
@@ -360,6 +380,11 @@
                 for part in range(parts):
                     to_group(d, part).wait_send()
 
+        @pl.when(z == groups - 1)
+        def _():
+            for part in range(parts):
+                to_first(part).wait_send()
+
     def own_sent(kind):
         for d in range(1, size):
             to_lead(d, kind).wait_send()
@@ -371,7 +396,7 @@
         @pl.when(z + d < groups)
         def _():
             def sent(kind):
-                for e in range(1, size):
+                for e in near(d):
                     to_peer(d, e, kind).wait_send()
 
             pieces(d, sent)
@@ -418,7 +443,7 @@
                 dma((parts,)), dma((parts,)),
                 dma((size,)), dma((size, parts)),
                 dma((size, parts)), dma((size,)),
-                dma((groups, parts)), dma((groups,)),
+                dma((groups, parts)), dma((groups,)), dma((parts,)), dma((1,)),
                 dma((groups, size)), dma((groups, size)),
                 dma((groups, parts)), dma((groups, parts)),
             ],

time: 27.3 us -> 26.5 us (0.971)
  Pallas kernels: 26.5 us -> 25.6 us
    pallas_call x1, Pallas kernels: 26.5 us -> 25.6 us  [shards(): pl.pallas_call(functools.partial(kernel, groups, size, parts), out_shape=...]
where the time goes in v9:
time: 26.5 us; the launch traced here: 26.3 us
  Pallas kernels  25.6 us (97%)
  local copies, waits for them, and re-layouts  0.71 us (3%)
    pallas_call x1, Pallas kernels, shards(): pl.pallas_call(functools.partial(kernel, groups, size, parts), out_shape=...  25.6 us
    unnamed x1, local copies, waits for them, and re-layouts  0.71 us

profile of v9, /device:TPU:1, one launch (start us, length us, event | category | flops | bytes accessed | tf_op | source)
XLA Modules:
  0.0 26.3 jit_solution(13315610667455167436)
XLA Ops:
  0.0 25.6 %shard_map.46 = f32[1,256,256]{2,1,0:T(8,128)S(1)} custom-call(f32[1,256,256]{2,1,0:T(8,128)} %x_hbm.1, f32[1,256]{1,0:T(1,128)} %mean_hbm.1, s32[1,128]{1,0:T(1,128)} %rows_hbm.1, f32[1,128]{1,0:T(1,128)} %prec_hbm.1), custom_call_target="tpu_custom_call" | custom-call | tf_op jit(solution)/shard_map/pallas_call | solution.py:424
  25.6 0.7 %copy.6 = f32[1,256,256]{2,1,0:T(8,128)} copy(f32[1,256,256]{2,1,0:T(8,128)S(1)} %shard_map.46) | data formatting | bytes 524288

commit v10 on v9

--- a/solution.py
+++ b/solution.py
@@ -247,7 +247,7 @@
     def spread(d):
         def act(kind):
             remote(piece(d, k, kind), z_send.at[d, 0], z_recv.at[d], (win, me)).wait_recv()
-            for e in near(d):
+            for e in reversed(near(d)):
                 to_peer(d, e, kind).start()
 
         pieces(d, act)
@@ -265,6 +265,11 @@
         for e in range(1, parts):
             to_sibling(d, e).start()
 
+    def apply(first, last):
+        for t in range(first, last):
+            later = unpacked([q_ref[part, t] for part in range(parts)])
+            v_ref[...] = dot3(split2(v_ref[...]), split2(later))
+
     def finish(d):
         for e in range(1, parts):
             part = lax.rem(me + parts - e, parts)
@@ -272,15 +277,13 @@
                 whole(d, part), gf_send.at[d, e], gf_recv.at[d, part], sibling(e)
             ).wait_recv()
         if d == 1:
-            for t in range(size):
-                later = unpacked([q_ref[part, t] for part in range(parts)])
-                v_ref[...] = dot3(split2(v_ref[...]), split2(later))
+            apply(0, size // 2)
         else:
             product = jnp.concatenate([p_ref[z + d, part] for part in range(parts)], axis=0)
             v_ref[...] = dot3(split2(v_ref[...]), split2(product))
 
     def send_own(kind):
-        for d in range(1, size):
+        for d in reversed(range(1, size)):
             to_lead(d, kind).start()
         pl.when(z > 0)(lambda: to_previous(kind).start())
 
@@ -300,9 +303,9 @@
 
     @pl.when(me == 0)
     def _():
-        for d in range(1, size):
+        for d in reversed(range(1, size)):
             src = flipped(k, d)
-            if d == size - 1:
+            if d == 1:
                 pl.when(z + 1 < groups)(functools.partial(spread, 1))
             for part in range(parts):
                 remote(
@@ -342,8 +345,8 @@
 
     @pl.when(me > 0)
     def _():
-        for d in range(1, size):
-            if d == size - 1:
+        for d in reversed(range(1, size)):
+            if d == 1:
                 pl.when(z + 1 < groups)(functools.partial(spread, 1))
             remote(tp_ref.at[flipped(k, d)], t_send.at[d], tf_recv.at[d], (win, me)).wait_recv()
             keep(d)
@@ -356,7 +359,9 @@
     pl.when(z + 1 < groups)(functools.partial(share, 1))
     for d in range(2, groups):
         pl.when(z + d < groups)(functools.partial(spread, d))
-    pl.when(z + 1 < groups)(functools.partial(finish, 1))
+        if d == 2:
+            pl.when(z + 1 < groups)(functools.partial(finish, 1))
+    pl.when(z + 1 < groups)(lambda: apply(size // 2, size))
     for d in range(2, groups):
         pl.when(z + d < groups)(functools.partial(share, d))
         if d > 2:

time: 26.5 us -> 27.2 us (1.026)
  Pallas kernels: 25.6 us -> 26.3 us
    pallas_call x1, Pallas kernels: 25.6 us -> 26.3 us  [shards(): pl.pallas_call(functools.partial(kernel, groups, size, parts), out_shape=...]
where the time goes in v10:
time: 27.2 us; the launch traced here: 27 us
  Pallas kernels  26.3 us (97%)
  local copies, waits for them, and re-layouts  0.71 us (3%)
    pallas_call x1, Pallas kernels, shards(): pl.pallas_call(functools.partial(kernel, groups, size, parts), out_shape=...  26.3 us
    unnamed x1, local copies, waits for them, and re-layouts  0.71 us

profile of v10, /device:TPU:1, one launch (start us, length us, event | category | flops | bytes accessed | tf_op | source)
XLA Modules:
  0.0 27.0 jit_solution(13856790604279411055)
XLA Ops:
  0.0 26.3 %shard_map.46 = f32[1,256,256]{2,1,0:T(8,128)S(1)} custom-call(f32[1,256,256]{2,1,0:T(8,128)} %x_hbm.1, f32[1,256]{1,0:T(1,128)} %mean_hbm.1, s32[1,128]{1,0:T(1,128)} %rows_hbm.1, f32[1,128]{1,0:T(1,128)} %prec_hbm.1), custom_call_target="tpu_custom_call" | custom-call | tf_op jit(solution)/shard_map/pallas_call | solution.py:429
  26.3 0.7 %copy.6 = f32[1,256,256]{2,1,0:T(8,128)} copy(f32[1,256,256]{2,1,0:T(8,128)S(1)} %shard_map.46) | data formatting | bytes 524288

commit v11 on v10

--- a/solution.py
+++ b/solution.py
@@ -265,11 +265,6 @@
         for e in range(1, parts):
             to_sibling(d, e).start()
 
-    def apply(first, last):
-        for t in range(first, last):
-            later = unpacked([q_ref[part, t] for part in range(parts)])
-            v_ref[...] = dot3(split2(v_ref[...]), split2(later))
-
     def finish(d):
         for e in range(1, parts):
             part = lax.rem(me + parts - e, parts)
@@ -277,7 +272,9 @@
                 whole(d, part), gf_send.at[d, e], gf_recv.at[d, part], sibling(e)
             ).wait_recv()
         if d == 1:
-            apply(0, size // 2)
+            for t in range(size):
+                later = unpacked([q_ref[part, t] for part in range(parts)])
+                v_ref[...] = dot3(split2(v_ref[...]), split2(later))
         else:
             product = jnp.concatenate([p_ref[z + d, part] for part in range(parts)], axis=0)
             v_ref[...] = dot3(split2(v_ref[...]), split2(product))
@@ -359,9 +356,7 @@
     pl.when(z + 1 < groups)(functools.partial(share, 1))
     for d in range(2, groups):
         pl.when(z + d < groups)(functools.partial(spread, d))
-        if d == 2:
-            pl.when(z + 1 < groups)(functools.partial(finish, 1))
-    pl.when(z + 1 < groups)(lambda: apply(size // 2, size))
+    pl.when(z + 1 < groups)(functools.partial(finish, 1))
     for d in range(2, groups):
         pl.when(z + d < groups)(functools.partial(share, d))
         if d > 2:

time: 27.2 us -> 26.8 us (0.985)
  Pallas kernels: 26.3 us -> 25.9 us
    pallas_call x1, Pallas kernels: 26.3 us -> 25.9 us  [shards(): pl.pallas_call(functools.partial(kernel, groups, size, parts), out_shape=...]
where the time goes in v11:
time: 26.8 us; the launch traced here: 26.6 us
  Pallas kernels  25.9 us (97%)
  local copies, waits for them, and re-layouts  0.71 us (3%)
    pallas_call x1, Pallas kernels, shards(): pl.pallas_call(functools.partial(kernel, groups, size, parts), out_shape=...  25.9 us
    unnamed x1, local copies, waits for them, and re-layouts  0.71 us

profile of v11, /device:TPU:1, one launch (start us, length us, event | category | flops | bytes accessed | tf_op | source)
XLA Modules:
  0.0 26.6 jit_solution(15415591844320171082)
XLA Ops:
  0.0 25.9 %shard_map.46 = f32[1,256,256]{2,1,0:T(8,128)S(1)} custom-call(f32[1,256,256]{2,1,0:T(8,128)} %x_hbm.1, f32[1,256]{1,0:T(1,128)} %mean_hbm.1, s32[1,128]{1,0:T(1,128)} %rows_hbm.1, f32[1,128]{1,0:T(1,128)} %prec_hbm.1), custom_call_target="tpu_custom_call" | custom-call | tf_op jit(solution)/shard_map/pallas_call | solution.py:424
  25.9 0.7 %copy.6 = f32[1,256,256]{2,1,0:T(8,128)} copy(f32[1,256,256]{2,1,0:T(8,128)S(1)} %shard_map.46) | data formatting | bytes 524288
